TPU v7x, 128 devices: a whole 4x4x4 slice. The times are simulated.
128 devices in a mesh: fsdp: 8 (over x, z_lo), sp: 16 (over z_hi, y, core).
Axes of the slice: x: 4, y: 4, z: 4 (z_hi: 2, z_lo: 2; z = z_hi * 2 + z_lo), core: 2. Of those that a mesh axis runs over, the one named last changes fastest.
Arguments:
- queries: bfloat16 [8, 2, 2048, 2048], P('fsdp', None, 'sp'), may hold values from -130 to 130
- span_keys: bfloat16 [8, 2, 2048, 512], P('fsdp', None, 'sp'), may hold values from -10 to 10
- span_values: bfloat16 [8, 2, 2048, 512], P('fsdp', None, 'sp'), may hold values from -18 to 18
- cotangent: bfloat16 [8, 2, 2048, 2048], P('fsdp', None, 'sp'), may hold values from -6 to 6
- cache_keys: bfloat16 [1024, 512], P('fsdp', 'sp'), may hold values from -9 to 9
- cache_values: bfloat16 [1024, 512], P('fsdp', 'sp'), may hold values from -18 to 18
- hist_count: int32 [8], replicated, may hold values from 1 to 2
- span_ids: int32 [8, 2], replicated, may hold values from 9 to 16
Outputs:
- attended_out: bfloat16 [8, 2, 2048, 2048], P('fsdp', None, 'sp')
- grad_queries: bfloat16 [8, 2, 2048, 2048], P('fsdp', None, 'sp')
- grad_keys: bfloat16 [8, 2, 2048, 512], P('fsdp', None, 'sp')
- grad_values: bfloat16 [8, 2, 2048, 512], P('fsdp', None, 'sp')
- grad_cache_keys: float32 [1024, 512], P('fsdp', 'sp')
- grad_cache_values: float32 [1024, 512], P('fsdp', 'sp')
All inputs are finite; a program needn't handle non-finite values.
Results may differ from a plain program's by a relative error of at most 0.019.
Values may be sent and summed in bfloat16 or wider, within the bound.
No kernel may reach another device: no remote copies, remote signals or barrier semaphores. Data moves between devices by JAX's collectives and lax.ppermute only.
A program may use at most 128 MiB of HBM per device.

v0:
```python
import math

import jax
import jax.numpy as jnp
from jax import lax
from jax.sharding import PartitionSpec as P

KVH = 4
HD = 128
SLOTS = 2
HB = 64


def from_partner(array, axis, stride):
    return lax.ppermute(array, axis, [(i, i ^ 1 << stride) for i in range(lax.axis_size(axis))])


def head_pass(query, key_rows, value_rows, grad_out, visible):
    score_scale = 1.0 / math.sqrt(query.shape[1])
    scores = jnp.dot(query, key_rows.T, preferred_element_type=jnp.float32) * score_scale
    scores = jnp.where(visible, scores, -jnp.inf)
    row_max = jnp.max(scores, axis=1, keepdims=True)
    weights = jnp.exp(scores - row_max)
    row_total = jnp.sum(weights, axis=1, keepdims=True)
    mixed = (
        jnp.dot(weights.astype(jnp.bfloat16), value_rows, preferred_element_type=jnp.float32)
        / row_total
    )
    attended = mixed.astype(jnp.bfloat16)
    log_total = row_max + jnp.log(row_total)
    row_delta = jnp.sum(
        grad_out.astype(jnp.float32) * attended.astype(jnp.float32), axis=1, keepdims=True
    )
    probability = jnp.exp(scores - log_total)
    grad_prob = jnp.dot(grad_out, value_rows.T, preferred_element_type=jnp.float32)
    grad_score = (probability * (grad_prob - row_delta)).astype(jnp.bfloat16)
    grad_query = (
        jnp.dot(grad_score, key_rows, preferred_element_type=jnp.float32) * score_scale
    ).astype(jnp.bfloat16)
    key_terms = jnp.dot(grad_score.T, query, preferred_element_type=jnp.float32) * score_scale
    value_terms = jnp.dot(
        probability.astype(jnp.bfloat16).T, grad_out, preferred_element_type=jnp.float32
    )
    return (attended, grad_query, key_terms, value_terms)


def join_history_pairs(stacked, levels):
    my_index = lax.axis_index("sp")
    for bit_number in range(levels):
        partner = from_partner(stacked, "sp", bit_number)
        is_lower = my_index >> bit_number & 1 == 0
        stacked = jnp.where(
            is_lower,
            jnp.concatenate([stacked, partner], axis=-1),
            jnp.concatenate([partner, stacked], axis=-1),
        )
    return stacked


def split_history_pairs(stacked, levels):
    my_index = lax.axis_index("sp")
    for bit_number in reversed(range(levels)):
        width_half = stacked.shape[-1] // 2
        is_lower = my_index >> bit_number & 1 == 0
        leading = stacked[..., :width_half]
        trailing = stacked[..., width_half:]
        retained = jnp.where(is_lower, leading, trailing)
        outgoing = jnp.where(is_lower, trailing, leading)
        stacked = retained + from_partner(outgoing, "sp", bit_number)
    return stacked


def history_visible(hist_count, span_id, hist_len, owner_total):
    row_ids = jnp.arange(hist_len, dtype=jnp.int32)
    owner_ids = row_ids // (hist_len // owner_total)
    slot_ids = row_ids // HB % SLOTS
    row_span = slot_ids * owner_total + owner_ids
    owners = jnp.arange(owner_total, dtype=jnp.int32)
    row_count = jnp.sum(
        jnp.where(owner_ids[:, None] == owners[None, :], hist_count[None, :], 0), axis=1
    )
    return (slot_ids < row_count) & (row_span < span_id)


def per_device(
    queries, span_keys, span_values, cotangent, cache_keys, cache_values, hist_count, span_ids
):
    sp_total = lax.axis_size("sp")
    owner_total = lax.axis_size("fsdp")
    member = lax.axis_index("fsdp")
    sharing = sp_total // KVH
    levels = sharing.bit_length() - 1
    tok_here = queries.shape[2]
    span_len = tok_here * sp_total
    query_local = queries[0]
    grad_local = cotangent[0]
    keys_send = jnp.broadcast_to(
        span_keys[0].reshape(2, tok_here, KVH, 1, HD), (2, tok_here, KVH, sharing, HD)
    ).reshape(2, tok_here, sp_total * HD)
    values_send = jnp.broadcast_to(
        span_values[0].reshape(2, tok_here, KVH, 1, HD), (2, tok_here, KVH, sharing, HD)
    ).reshape(2, tok_here, sp_total * HD)
    query_heads, grad_heads, keys_heads, values_heads = (
        lax.all_to_all(query_local, "sp", split_axis=2, concat_axis=1, tiled=True),
        lax.all_to_all(grad_local, "sp", split_axis=2, concat_axis=1, tiled=True),
        lax.all_to_all(keys_send, "sp", split_axis=2, concat_axis=1, tiled=True),
        lax.all_to_all(values_send, "sp", split_axis=2, concat_axis=1, tiled=True),
    )
    joined_hist = join_history_pairs(jnp.stack([cache_keys, cache_values]), levels)
    hist_keys, hist_values = (
        lax.all_gather(joined_hist[0], "fsdp", axis=0, tiled=True),
        lax.all_gather(joined_hist[1], "fsdp", axis=0, tiled=True),
    )
    hist_len = hist_keys.shape[0]
    block_rows = min(512, span_len)
    owners = jnp.arange(owner_total, dtype=jnp.int32)
    grad_hist_keys = jnp.zeros((hist_len, HD), jnp.float32)
    grad_hist_values = jnp.zeros((hist_len, HD), jnp.float32)
    attended_parts, grad_q_parts, grad_k_parts, grad_v_parts = ([], [], [], [])
    for ordinal in range(2):
        span_id = jnp.sum(jnp.where(owners == member, span_ids[:, ordinal], 0))
        visible_hist = history_visible(hist_count, span_id, hist_len, owner_total)
        own_keys = keys_heads[ordinal]
        own_values = values_heads[ordinal]
        sum_keys = jnp.zeros((span_len, HD), jnp.float32)
        sum_values = jnp.zeros((span_len, HD), jnp.float32)
        attended_heads, grad_q_heads = ([], [])
        query = query_heads[ordinal, :, 0:HD]
        grad_out = grad_heads[ordinal, :, 0:HD]
        attended_rows = []
        grad_q_rows = []
        for block in range(span_len // block_rows):
            start_row = block * block_rows
            end_row = start_row + block_rows
            key_rows = jnp.concatenate([hist_keys, own_keys[:end_row]], axis=0)
            value_rows = jnp.concatenate([hist_values, own_values[:end_row]], axis=0)
            causal = (start_row + jnp.arange(block_rows, dtype=jnp.int32))[:, None] >= jnp.arange(
                end_row, dtype=jnp.int32
            )[None, :]
            visible = jnp.concatenate(
                [jnp.broadcast_to(visible_hist[None, :], (block_rows, hist_len)), causal], axis=1
            )
            attended, grad_query, key_terms, value_terms = head_pass(
                query[start_row:end_row], key_rows, value_rows, grad_out[start_row:end_row], visible
            )
            attended_rows.append(attended)
            grad_q_rows.append(grad_query)
            grad_hist_keys = grad_hist_keys + key_terms[:hist_len]
            grad_hist_values = grad_hist_values + value_terms[:hist_len]
            sum_keys = sum_keys.at[:end_row].add(key_terms[hist_len:])
            sum_values = sum_values.at[:end_row].add(value_terms[hist_len:])
        attended_heads.append(jnp.concatenate(attended_rows, axis=0))
        grad_q_heads.append(jnp.concatenate(grad_q_rows, axis=0))
        attended_parts.append(attended_heads[0])
        grad_q_parts.append(grad_q_heads[0])
        grad_k_parts.append(sum_keys)
        grad_v_parts.append(sum_values)
    attended_tokens, grad_q_tokens = (
        lax.all_to_all(jnp.stack(attended_parts), "sp", split_axis=1, concat_axis=2, tiled=True),
        lax.all_to_all(jnp.stack(grad_q_parts), "sp", split_axis=1, concat_axis=2, tiled=True),
    )
    key_partial = jnp.stack(grad_k_parts)
    value_partial = jnp.stack(grad_v_parts)
    keys_back, values_back = (
        lax.all_to_all(key_partial, "sp", split_axis=1, concat_axis=2, tiled=True),
        lax.all_to_all(value_partial, "sp", split_axis=1, concat_axis=2, tiled=True),
    )
    grad_k_tokens = (
        jnp.sum(keys_back.reshape(2, tok_here, KVH, sharing, HD), axis=3)
        .reshape(2, tok_here, KVH * HD)
        .astype(jnp.bfloat16)
    )
    grad_v_tokens = (
        jnp.sum(values_back.reshape(2, tok_here, KVH, sharing, HD), axis=3)
        .reshape(2, tok_here, KVH * HD)
        .astype(jnp.bfloat16)
    )
    owned_keys, owned_values = (
        lax.psum_scatter(grad_hist_keys, "fsdp", scatter_dimension=0, tiled=True),
        lax.psum_scatter(grad_hist_values, "fsdp", scatter_dimension=0, tiled=True),
    )
    split_owned = split_history_pairs(jnp.stack([owned_keys, owned_values]), levels)
    grad_cache_keys = split_owned[0]
    grad_cache_values = split_owned[1]
    return (
        attended_tokens[None],
        grad_q_tokens[None],
        grad_k_tokens[None],
        grad_v_tokens[None],
        grad_cache_keys,
        grad_cache_values,
    )


def solution(mesh):
    placed = (
        P("fsdp", None, "sp", None),
        P("fsdp", None, "sp", None),
        P("fsdp", None, "sp", None),
        P("fsdp", None, "sp", None),
        P("fsdp", "sp"),
        P("fsdp", "sp"),
        P(),
        P(),
    )
    return jax.shard_map(
        per_device,
        mesh=mesh,
        in_specs=placed,
        out_specs=(
            P("fsdp", None, "sp", None),
            P("fsdp", None, "sp", None),
            P("fsdp", None, "sp", None),
            P("fsdp", None, "sp", None),
            P("fsdp", "sp"),
            P("fsdp", "sp"),
        ),
        check_vma=False,
    )
```

profile of v0, /device:TPU:1, one launch (start us, length us, event | category | flops | bytes accessed | tf_op | source)
XLA Modules:
  0.0 435.5 jit_solution(8846766848586949616)
XLA Ops:
  8.1 1.5 collective-permute-start
  10.7 1.8 broadcast_in_dim.65
  12.5 8.0 %all-to-all-start.2 = ((bf16[2,128,2048]{1,0,2:T(2,128)(2,1)}), bf16[2,128,2048]{1,0,2:T(2,128)(2,1)S(1)}, u32[]{:S(2)}, u32[]{:S(2)}) async-start(bf16[2,128,2048]{1,0,2:T(2,128)(2,1)} %bitcast.16), calls=%async_computation.2 | async-start | bytes 2097152 | tf_op jit(solution)/shard_map/all_to_all | solution.py:107
  22.6 1.5 iota_compare_fusion.1
  24.1 1.9 iota_compare_fusion
  25.9 11.9 %all-to-all-done.2 = bf16[2,128,2048]{1,0,2:T(2,128)(2,1)S(1)} async-done(((bf16[2,128,2048]{1,0,2:T(2,128)(2,1)}), bf16[2,128,2048]{1,0,2:T(2,128)(2,1)S(1)}, u32[]{:S(2)}, u32[]{:S(2)}) %all-to-all-start.2) | async-done | bytes 1048608 | tf_op jit(solution)/shard_map/all_to_all | solution.py:107
  37.8 1.8 broadcast_in_dim.62
  39.7 4.2 all-to-all-start
  45.3 1.5 collective-permute-start.1
  47.5 3.7 copy.166
  51.2 3.7 copy.195
  54.9 4.0 collective-permute-done.1
  59.0 22.2 %all-gather.1 = bf16[1,1024,128]{2,1,0:T(8,128)(2,1)S(1)} all-gather(bf16[1,128,128]{2,1,0:T(8,128)(2,1)S(1)} %get-tuple-element.310), channel_id=3, replica_groups=mesh['fsdp'=8,'sp'=16] {'fsdp'}, dimensions={1}, use_global_device_ids=true | all-gather | bytes 294912 | tf_op jit(solution)/shard_map/all_gather | solution.py:112
  81.1 13.6 %all-to-all-start.1 = ((bf16[2,128,2048]{1,0,2:T(2,128)(2,1)}), bf16[2,128,2048]{1,0,2:T(2,128)(2,1)}, u32[]{:S(2)}, u32[]{:S(2)}) async-start(bf16[2,128,2048]{1,0,2:T(2,128)(2,1)} %bitcast.9), calls=%async_computation.1 | async-start | bytes 2097152 | tf_op jit(solution)/shard_map/all_to_all | solution.py:104
  94.8 29.3 %all-gather = bf16[1,1024,128]{2,1,0:T(8,128)(2,1)} all-gather(bf16[1,128,128]{2,1,0:T(8,128)(2,1)S(1)} %get-tuple-element.311), channel_id=2, replica_groups=mesh['fsdp'=8,'sp'=16] {'fsdp'}, dimensions={1}, use_global_device_ids=true | all-gather | bytes 294912 | tf_op jit(solution)/shard_map/all_gather | solution.py:111
  129.0 17.2 %all-to-all-start.4 = ((bf16[2,128,2048]{1,0,2:T(2,128)(2,1)}), bf16[2,128,2048]{1,0,2:T(2,128)(2,1)S(1)}, u32[]{:S(2)}, u32[]{:S(2)}) async-start(bf16[2,128,2048]{1,0,2:T(2,128)(2,1)} %bitcast.56), calls=%async_computation.4 | async-start | bytes 2097152 | tf_op jit(solution)/shard_map/all_to_all | solution.py:105
  153.2 10.3 %all-to-all-done.4 = bf16[2,128,2048]{1,0,2:T(2,128)(2,1)S(1)} async-done(((bf16[2,128,2048]{1,0,2:T(2,128)(2,1)}), bf16[2,128,2048]{1,0,2:T(2,128)(2,1)S(1)}, u32[]{:S(2)}, u32[]{:S(2)}) %all-to-all-start.4) | async-done | bytes 1048608 | tf_op jit(solution)/shard_map/all_to_all | solution.py:105
  165.7 1.8 fusion.213
  172.0 1.5 convolution_multiply_fusion.6
  179.8 1.5 convolution_multiply_fusion.7
  181.9 2.1 fusion.216
  186.1 2.0 fusion.66
  190.5 1.7 convolution_multiply_fusion.9
  193.5 2.5 fusion.215
  196.8 1.6 multiply_reduce_fusion.5
  198.4 1.9 fusion.54
  201.4 1.6 fusion.110
  203.0 1.9 convolution_multiply_fusion.1
  206.4 2.8 fusion.210
  210.1 2.2 multiply_reduce_fusion
  212.3 2.1 fusion.32
  215.7 1.7 fusion.113
  217.4 2.2 convolution_multiply_fusion.2
  219.6 1.9 copy.186
  221.4 1.8 copy.184
  225.5 2.1 copy.189
  227.6 1.7 copy.188
  229.3 1.7 copy.185
  233.3 1.9 fusion.212
  237.1 1.7 fusion.64
  245.2 1.9 fusion.52
  248.3 1.6 fusion.111
  252.9 1.7 copy-done
  256.0 9.5 %copy.193 = bf16[2,2048,128]{2,0,1:T(2,128)(2,1)} copy(bf16[2,2048,128]{2,1,0:T(8,128)(2,1)S(1)} %pad_maximum_fusion.2) | data formatting | bytes 2097152 | tf_op jit(solution)/shard_map/stack | solution.py:159
  265.5 5.2 %all-to-all-start.3 = ((bf16[2,2048,128]{2,0,1:T(2,128)(2,1)}), bf16[2,2048,128]{2,0,1:T(2,128)(2,1)}, u32[]{:S(2)}, u32[]{:S(2)}) async-start(bf16[2,2048,128]{2,0,1:T(2,128)(2,1)} %copy.193), calls=%async_computation.3 | async-start | bytes 2097152 | tf_op jit(solution)/shard_map/all_to_all | solution.py:159
  270.7 3.9 fusion.34
  278.4 9.5 %copy.197 = bf16[2,2048,128]{2,0,1:T(2,128)(2,1)} copy(bf16[2,2048,128]{2,1,0:T(8,128)(2,1)S(1)} %pad_maximum_fusion.3) | data formatting | bytes 2097152 | tf_op jit(solution)/shard_map/stack | solution.py:160
  290.0 7.4 %all-to-all-start.5 = ((bf16[2,2048,128]{2,0,1:T(2,128)(2,1)}), bf16[2,2048,128]{2,0,1:T(2,128)(2,1)}, u32[]{:S(2)}, u32[]{:S(2)}) async-start(bf16[2,2048,128]{2,0,1:T(2,128)(2,1)} %copy.197), calls=%async_computation.5 | async-start | bytes 2097152 | tf_op jit(solution)/shard_map/all_to_all | solution.py:160
  299.7 9.0 %copy.202 = f32[2,2048,128]{2,0,1:T(2,128)} copy(f32[2,2048,128]{2,1,0:T(8,128)S(1)} %pad_maximum_fusion.1) | data formatting | bytes 4194304 | tf_op jit(solution)/shard_map/stack | solution.py:163
  308.8 1.9 convolution_multiply_fusion
  310.7 1.7 convolution_multiply_fusion.8
  312.9 2.1 convolution_multiply_fusion.3
  315.1 7.5 %all-to-all-start.7 = ((f32[2,2048,128]{2,0,1:T(2,128)}), f32[2,2048,128]{2,0,1:T(2,128)}, u32[]{:S(2)}, u32[]{:S(2)}) async-start(f32[2,2048,128]{2,0,1:T(2,128)} %copy.202), calls=%async_computation.7 | async-start | bytes 4194304 | tf_op jit(solution)/shard_map/all_to_all | solution.py:166
  322.7 3.8 slice_add_fusion.15
  326.5 1.6 fusion.150
  328.9 8.6 %copy.199 = f32[2,2048,128]{2,0,1:T(2,128)} copy(f32[2,2048,128]{2,1,0:T(8,128)S(1)} %pad_maximum_fusion) | data formatting | bytes 4194304 | tf_op jit(solution)/shard_map/stack | solution.py:162
  337.5 17.6 %all-to-all-done.7 = f32[2,2048,128]{2,0,1:T(2,128)} async-done(((f32[2,2048,128]{2,0,1:T(2,128)}), f32[2,2048,128]{2,0,1:T(2,128)}, u32[]{:S(2)}, u32[]{:S(2)}) %all-to-all-start.7) | async-done | bytes 2097184 | tf_op jit(solution)/shard_map/all_to_all | solution.py:166
  355.1 3.8 all-to-all-start.6
  358.9 43.8 %reduce-scatter.3.cloned.1.call-done = f32[128,128]{1,0:T(8,128)} async-done(((f32[1024,128]{1,0:T(8,128)}), f32[128,128]{1,0:T(8,128)}) %reduce-scatter.3.cloned.1.call-update) | async-done | bytes 65552 | tf_op jit(solution)/shard_map/reduce_scatter | solution.py:179
  405.2 2.5 collective-permute-done.2
  408.8 5.6 %collective-permute-start.3 = (f32[2,128,32]{2,1,0:T(8,128)S(1)}, f32[2,128,32]{2,1,0:T(8,128)S(1)}, u32[]{:S(2)}, u32[]{:S(2)}) collective-permute-start(f32[2,128,32]{2,1,0:T(8,128)S(1)} %slice_select_fusion), channel_id=1, source_target_pairs={{0,1},{1,0},{2,3},{3,2},{4,5},{5,4},{6,7},{7,6},{8,9},{9,8},{10,11... | collective-permute-start | bytes 98312 | tf_op jit(solution)/shard_map/ppermute | solution.py:15
  414.4 1.9 copy.194
  417.6 1.9 copy.198
  422.3 2.7 reduce.37
  (333 shorter events, 81.8 us)
Async XLA Ops:
  7.2 14.5 %copy-start.91 = (s32[8,2]{0,1:T(2,128)S(1)}, s32[8,2]{0,1:T(2,128)}, u32[]{:S(2)}) copy-start(s32[8,2]{0,1:T(2,128)} %param.55) | copy-start | bytes 196
  7.2 15.2 %copy-start.92 = (s32[8]{0:T(128)S(1)}, s32[8]{0:T(128)}, u32[]{:S(2)}) copy-start(s32[8]{0:T(128)} %param.54) | copy-start | bytes 100
  7.2 15.2 %copy-start.71 = (bf16[1,2,128,512]{3,2,1,0:T(8,128)(2,1)S(1)}, bf16[1,2,128,512]{3,2,1,0:T(8,128)(2,1)}, u32[]{:S(2)}) copy-start(bf16[1,2,128,512]{3,2,1,0:T(8,128)(2,1)} %param.49) | copy-start | bytes 786436
  8.1 37.1 %collective-permute-start = (bf16[2,128,32]{2,1,0:T(8,128)(2,1)S(1)}, bf16[2,128,32]{2,1,0:T(8,128)(2,1)S(1)}, u32[]{:S(2)}, u32[]{:S(2)}) collective-permute-start(bf16[2,128,32]{2,1,0:T(8,128)(2,1)S(1)} %copy.161), channel_id=1, source_target_pairs={{0,1},{1,0},{2,3},{3,2},{4,5},{5,4},{6,7},{7,6},{8,9},{9,8},{10,11... | collective-permute-start | bytes 49160 | tf_op jit(solution)/shard_map/ppermute | solution.py:15
  12.5 25.4 %all-to-all-start.2 = ((bf16[2,128,2048]{1,0,2:T(2,128)(2,1)}), bf16[2,128,2048]{1,0,2:T(2,128)(2,1)S(1)}, u32[]{:S(2)}, u32[]{:S(2)}) async-start(bf16[2,128,2048]{1,0,2:T(2,128)(2,1)} %bitcast.16), calls=%async_computation.2 | async-start | bytes 2097152 | tf_op jit(solution)/shard_map/all_to_all | solution.py:107
  39.7 41.5 %all-to-all-start = ((bf16[2,128,2048]{1,0,2:T(2,128)(2,1)}), bf16[2,128,2048]{1,0,2:T(2,128)(2,1)S(1)}, u32[]{:S(2)}, u32[]{:S(2)}) async-start(bf16[2,128,2048]{1,0,2:T(2,128)(2,1)} %bitcast.5), calls=%async_computation | async-start | bytes 2097152 | tf_op jit(solution)/shard_map/all_to_all | solution.py:106
  45.3 13.6 %collective-permute-start.1 = (bf16[2,128,64]{2,1,0:T(8,128)(2,1)S(1)}, bf16[2,128,64]{2,1,0:T(8,128)(2,1)S(1)}, u32[]{:S(2)}, u32[]{:S(2)}) collective-permute-start(bf16[2,128,64]{2,1,0:T(8,128)(2,1)S(1)} %maximum_select_fusion), channel_id=1, source_target_pairs={{0,2},{1,3},{2,0},{3,1},{4,6},{5,7},{6,4},{7,5},{8,10},{9,11},{10,... | collective-permute-start | bytes 98312 | tf_op jit(solution)/shard_map/ppermute | solution.py:15
  81.1 47.9 %all-to-all-start.1 = ((bf16[2,128,2048]{1,0,2:T(2,128)(2,1)}), bf16[2,128,2048]{1,0,2:T(2,128)(2,1)}, u32[]{:S(2)}, u32[]{:S(2)}) async-start(bf16[2,128,2048]{1,0,2:T(2,128)(2,1)} %bitcast.9), calls=%async_computation.1 | async-start | bytes 2097152 | tf_op jit(solution)/shard_map/all_to_all | solution.py:104
  129.0 34.5 %all-to-all-start.4 = ((bf16[2,128,2048]{1,0,2:T(2,128)(2,1)}), bf16[2,128,2048]{1,0,2:T(2,128)(2,1)S(1)}, u32[]{:S(2)}, u32[]{:S(2)}) async-start(bf16[2,128,2048]{1,0,2:T(2,128)(2,1)} %bitcast.56), calls=%async_computation.4 | async-start | bytes 2097152 | tf_op jit(solution)/shard_map/all_to_all | solution.py:105
  152.1 13.6 %copy-start.51 = (bf16[1,4,128,128]{3,2,1,0:T(8,128)(2,1)S(1)}, bf16[1,4,128,128]{3,2,1,0:T(8,128)(2,1)}, u32[]{:S(2)}) copy-start(bf16[1,4,128,128]{3,2,1,0:T(8,128)(2,1)} %copy.182) | copy-start | bytes 393220
  152.1 13.6 %copy-start.64 = (bf16[1,1024,128]{2,1,0:T(8,128)(2,1)S(1)}, bf16[1,1024,128]{2,1,0:T(8,128)(2,1)}, u32[]{:S(2)}) copy-start(bf16[1,1024,128]{2,1,0:T(8,128)(2,1)} %all-gather) | copy-start | bytes 786436
  152.1 13.6 %copy-start.88 = (bf16[1,4,128,128]{3,2,1,0:T(8,128)(2,1)S(1)}, bf16[1,4,128,128]{3,2,1,0:T(8,128)(2,1)}, u32[]{:S(2)}) copy-start(bf16[1,4,128,128]{3,2,1,0:T(8,128)(2,1)} %copy.181) | copy-start | bytes 393220
  165.7 2.4 copy-start.53
  165.7 2.3 copy-start.49
  170.0 61.7 %copy-start.18 = (f32[1536,128]{1,0:T(8,128)}, f32[1536,128]{1,0:T(8,128)S(1)}, u32[]{:S(2)}) copy-start(f32[1536,128]{1,0:T(8,128)S(1)} %fusion.76) | copy-start | bytes 2359300
  170.7 2.8 copy-start.60
  170.7 2.9 copy-start.61
  170.7 3.1 copy-start.50
  170.7 3.5 copy-start.72
  177.3 54.5 %copy-start.20 = (f32[1536,128]{1,0:T(8,128)}, f32[1536,128]{1,0:T(8,128)S(1)}, u32[]{:S(2)}) copy-start(f32[1536,128]{1,0:T(8,128)S(1)} %fusion.78) | copy-start | bytes 2359300
  178.6 2.8 copy-start.36
  178.6 3.0 copy-start.37
  178.6 3.2 copy-start.48
  181.7 2.3 copy-start.74
  189.1 3.1 copy-start.29
  189.1 4.0 copy-start.30
  190.5 2.9 copy-start.47
  203.0 2.9 copy-start.27
  203.0 3.2 copy-start.46
  217.4 5.9 %copy-start.25 = (bf16[1,16,128,128]{2,3,1,0:T(8,128)(2,1)S(1)}, bf16[1,16,128,128]{2,3,1,0:T(8,128)(2,1)}, u32[]{:S(2)}) copy-start(bf16[1,16,128,128]{2,3,1,0:T(8,128)(2,1)} %get-tuple-element.306) | copy-start | bytes 1572868
  217.4 6.9 %copy-start.28 = (bf16[1,12,128,128]{2,3,1,0:T(8,128)(2,1)S(1)}, bf16[1,12,128,128]{2,3,1,0:T(8,128)(2,1)}, u32[]{:S(2)}) copy-start(bf16[1,12,128,128]{2,3,1,0:T(8,128)(2,1)} %get-tuple-element.303) | copy-start | bytes 1179652
  219.6 5.6 %copy-start.24 = (bf16[1,16,128,128]{2,3,1,0:T(8,128)(2,1)S(1)}, bf16[1,16,128,128]{2,3,1,0:T(8,128)(2,1)}, u32[]{:S(2)}) copy-start(bf16[1,16,128,128]{2,3,1,0:T(8,128)(2,1)} %get-tuple-element.304) | copy-start | bytes 1572868
  219.6 11.4 %copy-start.41 = (bf16[1,4,128,128]{2,3,1,0:T(8,128)(2,1)S(1)}, bf16[1,4,128,128]{2,3,1,0:T(8,128)(2,1)}, u32[]{:S(2)}) copy-start(bf16[1,4,128,128]{2,3,1,0:T(8,128)(2,1)} %get-tuple-element.293) | copy-start | bytes 393220
  225.5 27.4 %copy-start.22 = (bf16[1,16,128,128]{3,2,1,0:T(8,128)(2,1)}, bf16[1,16,128,128]{3,2,1,0:T(8,128)(2,1)S(1)}, u32[]{:S(2)}) copy-start(bf16[1,16,128,128]{3,2,1,0:T(8,128)(2,1)S(1)} %copy.180) | copy-start | bytes 1572868
  248.3 2.4 copy-start.56
  248.3 2.5 copy-start.57
  252.0 2.6 copy-start
  256.0 18.6 %slice-start = ((s8[6291456]{0:T(1024)(128)(4,1)}), s8[2097152]{0:T(1024)(128)(4,1)S(1)}, s32[]{:S(2)}) async-start(s8[6291456]{0:T(1024)(128)(4,1)} %bitcast.217), calls=%async_computation.12 | async-start | bytes 4194304
  265.5 24.5 %all-to-all-start.3 = ((bf16[2,2048,128]{2,0,1:T(2,128)(2,1)}), bf16[2,2048,128]{2,0,1:T(2,128)(2,1)}, u32[]{:S(2)}, u32[]{:S(2)}) async-start(bf16[2,2048,128]{2,0,1:T(2,128)(2,1)} %copy.193), calls=%async_computation.3 | async-start | bytes 2097152 | tf_op jit(solution)/shard_map/all_to_all | solution.py:159
  270.7 4.0 slice-start.1
  270.7 4.1 copy-start.23
  276.1 11.7 %copy-start.17 = (f32[2048,128]{1,0:T(8,128)S(1)}, f32[2048,128]{1,0:T(8,128)}, u32[]{:S(2)}) copy-start(f32[2048,128]{1,0:T(8,128)} %fusion.64) | copy-start | bytes 3145732
  276.1 11.7 %copy-start.19 = (f32[1536,128]{1,0:T(8,128)S(1)}, f32[1536,128]{1,0:T(8,128)}, u32[]{:S(2)}) copy-start(f32[1536,128]{1,0:T(8,128)} %copy-done.18) | copy-start | bytes 2359300
  276.2 11.7 %copy-start.21 = (f32[1536,128]{1,0:T(8,128)S(1)}, f32[1536,128]{1,0:T(8,128)}, u32[]{:S(2)}) copy-start(f32[1536,128]{1,0:T(8,128)} %copy-done.20) | copy-start | bytes 2359300
  278.2 9.7 %copy-start.5 = (f32[2048,128]{1,0:T(8,128)S(1)}, f32[2048,128]{1,0:T(8,128)}, u32[]{:S(2)}) copy-start(f32[2048,128]{1,0:T(8,128)} %scatter-add.50) | copy-start | bytes 3145732
  278.2 9.7 %copy-start.13 = (f32[3072,128]{1,0:T(8,128)S(1)}, f32[3072,128]{1,0:T(8,128)}, u32[]{:S(2)}) copy-start(f32[3072,128]{1,0:T(8,128)} %fusion.32) | copy-start | bytes 4718596
  278.2 9.7 %copy-start.14 = (f32[2560,128]{1,0:T(8,128)S(1)}, f32[2560,128]{1,0:T(8,128)}, u32[]{:S(2)}) copy-start(f32[2560,128]{1,0:T(8,128)} %fusion.54) | copy-start | bytes 3932164
  278.2 9.7 %copy-start.15 = (f32[2560,128]{1,0:T(8,128)S(1)}, f32[2560,128]{1,0:T(8,128)}, u32[]{:S(2)}) copy-start(f32[2560,128]{1,0:T(8,128)} %fusion.52) | copy-start | bytes 3932164
  278.2 9.7 %copy-start.16 = (f32[2048,128]{1,0:T(8,128)S(1)}, f32[2048,128]{1,0:T(8,128)}, u32[]{:S(2)}) copy-start(f32[2048,128]{1,0:T(8,128)} %fusion.66) | copy-start | bytes 3145732
  289.9 7.7 %slice-start.2 = ((f32[1536,128]{1,0:T(8,128)}), f32[512,128]{1,0:T(8,128)S(1)}, s32[]{:S(2)}) async-start(f32[1536,128]{1,0:T(8,128)} %convolution_multiply_fusion.6), calls=%async_computation.14 | async-start | bytes 524288 | tf_op jit(solution)/shard_map/slice | solution.py:150
  290.0 25.1 %all-to-all-start.5 = ((bf16[2,2048,128]{2,0,1:T(2,128)(2,1)}), bf16[2,2048,128]{2,0,1:T(2,128)(2,1)}, u32[]{:S(2)}, u32[]{:S(2)}) async-start(bf16[2,2048,128]{2,0,1:T(2,128)(2,1)} %copy.197), calls=%async_computation.5 | async-start | bytes 2097152 | tf_op jit(solution)/shard_map/all_to_all | solution.py:160
  297.4 61.5 %reduce-scatter.5.cloned.1.call-start = ((), (), s32[]{:S(2)}) async-start(), calls=%async_computation.11 | async-start | bytes 589824 | tf_op jit(solution)/shard_map/reduce_scatter | solution.py:180
  298.7 10.0 %copy-start.4 = (bf16[512,2560]{0,1:T(8,128)(2,1)S(1)}, bf16[512,2560]{0,1:T(8,128)(2,1)}, u32[]{:S(2)}) copy-start(bf16[512,2560]{0,1:T(8,128)(2,1)} %copy-done.3) | copy-start | bytes 7864324
  298.7 10.1 %copy-start.45 = (bf16[1,4,128,128]{3,2,1,0:T(8,128)(2,1)S(1)}, bf16[1,4,128,128]{3,2,1,0:T(8,128)(2,1)}, u32[]{:S(2)}) copy-start(bf16[1,4,128,128]{3,2,1,0:T(8,128)(2,1)} %copy.188) | copy-start | bytes 393220
  310.7 2.3 copy-start.2
  310.7 2.3 copy-start.40
  315.1 7.6 %copy-start.6 = (f32[2048,128]{1,0:T(8,128)S(1)}, f32[2048,128]{1,0:T(8,128)}, u32[]{:S(2)}) copy-start(f32[2048,128]{1,0:T(8,128)} %scatter-add.45) | copy-start | bytes 3145732
  315.1 7.6 %copy-start.7 = (f32[2048,128]{1,0:T(8,128)S(1)}, f32[2048,128]{1,0:T(8,128)}, u32[]{:S(2)}) copy-start(f32[2048,128]{1,0:T(8,128)} %scatter-add.40) | copy-start | bytes 3145732
  315.1 7.6 %copy-start.10 = (f32[2560,128]{1,0:T(8,128)S(1)}, f32[2560,128]{1,0:T(8,128)}, u32[]{:S(2)}) copy-start(f32[2560,128]{1,0:T(8,128)} %convolution_multiply_fusion.1) | copy-start | bytes 3932164
  315.1 40.0 %all-to-all-start.7 = ((f32[2,2048,128]{2,0,1:T(2,128)}), f32[2,2048,128]{2,0,1:T(2,128)}, u32[]{:S(2)}, u32[]{:S(2)}) async-start(f32[2,2048,128]{2,0,1:T(2,128)} %copy.202), calls=%async_computation.7 | async-start | bytes 4194304 | tf_op jit(solution)/shard_map/all_to_all | solution.py:166
  322.6 80.1 %reduce-scatter.3.cloned.1.call-start = ((), (), s32[]{:S(2)}) async-start(), calls=%async_computation.10 | async-start | bytes 589824 | tf_op jit(solution)/shard_map/reduce_scatter | solution.py:179
  355.1 71.0 %all-to-all-start.6 = ((f32[2,2048,128]{2,0,1:T(2,128)}), f32[2,2048,128]{2,0,1:T(2,128)S(1)}, u32[]{:S(2)}, u32[]{:S(2)}) async-start(f32[2,2048,128]{2,0,1:T(2,128)} %copy.199), calls=%async_computation.6 | async-start | bytes 4194304 | tf_op jit(solution)/shard_map/all_to_all | solution.py:165
  403.8 3.9 collective-permute-start.2
  408.8 12.0 %collective-permute-start.3 = (f32[2,128,32]{2,1,0:T(8,128)S(1)}, f32[2,128,32]{2,1,0:T(8,128)S(1)}, u32[]{:S(2)}, u32[]{:S(2)}) collective-permute-start(f32[2,128,32]{2,1,0:T(8,128)S(1)} %slice_select_fusion), channel_id=1, source_target_pairs={{0,1},{1,0},{2,3},{3,2},{4,5},{5,4},{6,7},{7,6},{8,9},{9,8},{10,11... | collective-permute-start | bytes 98312 | tf_op jit(solution)/shard_map/ppermute | solution.py:15
  (47 other events, 66.8 us)
Sparse Core Ops, SparseCore 0:
  308.8 46.5 reduce-scatter.4
  358.6 44.1 reduce-scatter.2
where the time goes:
time: 443 us; the launch traced here: 436 us
  local copies, waits for them, and re-layouts  99.4 us (22%)
  waiting for transfers between devices  90.1 us (20%)
  starting transfers between devices  77 us (17%)
  matrix products  73.5 us (17%)
  blocking collectives  51.5 us (12%)
  other arithmetic  28.6 us (6%)
  between operations  15.6 us (4%)
    reduce_scatter x1, waiting for transfers between devices, per_device(): lax.psum_scatter(grad_hist_keys, 'fsdp', scatter_dimension=0, tiled=True)  43.8 us
    all_gather x1, blocking collectives, per_device(): lax.all_gather(joined_hist[0], 'fsdp', axis=0, tiled=True)  29.3 us
    all_gather x1, blocking collectives, per_device(): lax.all_gather(joined_hist[1], 'fsdp', axis=0, tiled=True)  22.2 us
    unnamed x196, local copies, waits for them, and re-layouts  17.8 us
    all_to_all x1, waiting for transfers between devices, per_device(): lax.all_to_all(value_partial, 'sp', split_axis=1, concat_axis=2, tiled=True)  17.6 us
    all_to_all x1, starting transfers between devices, per_device(): lax.all_to_all(grad_local, 'sp', split_axis=2, concat_axis=1, tiled=True)  17.2 us
    dot_general x8, matrix products, head_pass(): jnp.dot(probability.astype(jnp.bfloat16).T, grad_out, preferred_element_t...  14.7 us
    dot_general x8, matrix products, head_pass(): jnp.dot(grad_score.T, query, preferred_element_type=jnp.float32)  14.5 us
  transfers between devices with their start and end apart: 14, of which 6 were waited for; matrix products, arithmetic and copies ran while one was open for 22% of the time, Pallas kernels for 0%

commit v1 on v0

v1 whole, which is shorter than its diff:
```python
import functools
import math

import jax
import jax.numpy as jnp
from jax import lax
from jax.experimental import pallas as pl
from jax.experimental.pallas import tpu as pltpu
from jax.sharding import Mesh
from jax.sharding import PartitionSpec as P

BF = jnp.bfloat16
F32 = jnp.float32
HEADS = 4
KVH = 4
D = 128
TB = 128
ROWS = HEADS * TB
CK = 256
HIST = 1024
SPAN = 2048
NROW = HIST + SPAN
NCH = NROW // CK
SCALE = 1.0 / math.sqrt(D)
C2 = SCALE * math.log2(math.e)
NEG = -1e30
STEP1, STEP2, STEP3 = 4, 4, 4
SP = ("zhi", "y", "core")
FS = ("x", "zlo")


def dg(a, b, ca, cb):
    return lax.dot_general(a, b, (((ca,), (cb,)), ((), ())), preferred_element_type=F32)


def pieces(x):
    a = x.astype(BF)
    r = x - a.astype(F32)
    b = r.astype(BF)
    c = (r - b.astype(F32)).astype(BF)
    return a, b, c


def at_cols(x, rows):
    ln = lax.broadcasted_iota(jnp.int32, (rows, D), 1)
    out = jnp.zeros((rows, D), F32)
    for k, p in enumerate(pieces(x)):
        out = jnp.where(ln == k, p.astype(F32), out)
    return out


def span_kernel(
    ordinal, last, pos_ref, cnt_ref, ids_ref, qg0, qg1, qg2, qg3, kv0, kv1, kv2, kv3, hist_ref, *rest
):
    if last:
        acc_ref, *rest = rest
    (att_ref, dq_ref, dkv_ref, hg_ref, ks, vs, q_s, ga_s, qt_s, gt_s, s_s, w_s, mx, o_s, dq_s, dkt, dvt, kt, vt) = rest
    zhi, y_me, core, f_me = pos_ref[0], pos_ref[1], pos_ref[2], pos_ref[3]
    qg_refs = (qg0, qg1, qg2, qg3)
    kv_refs = (kv0, kv1, kv2, kv3)
    span_id = ids_ref[f_me, ordinal]
    see = [(cnt_ref[f] > 1) & (f + 8 < span_id) for f in range(8)]
    vs[:, D:] = jnp.ones((NROW, D), BF)
    n1 = jnp.int32(0)
    for f in range(8):
        n1 = n1 + see[f].astype(jnp.int32)
    nh1 = (n1 + 3) // 4
    ln = lax.broadcasted_iota(jnp.int32, (HIST, D), 1)
    rw = lax.broadcasted_iota(jnp.int32, (HIST, D), 0)
    ks[0:HIST, D:] = jnp.where((ln == 0) & (rw >= 512 + n1 * 64), NEG, 0.0).astype(BF)
    base = pl.multiple_of(512 + nh1 * CK, CK)
    zc = zhi * 2 + core
    n = jnp.int32(0)
    for f in range(8):
        rows = jnp.concatenate(
            [hist_ref[f, lax.rem(zc - p + 4, 4), i] for i in range(2) for p in range(4)], axis=0
        ).T
        ks[f * 64 : (f + 1) * 64, 0:D] = rows[0:64, 0:D]
        vs[f * 64 : (f + 1) * 64, 0:D] = rows[0:64, D:]
        at = pl.multiple_of(512 + n * 64, 64)
        ks[pl.ds(at, 64), 0:D] = rows[64:, 0:D]
        vs[pl.ds(at, 64), 0:D] = rows[64:, D:]
        n = n + see[f].astype(jnp.int32)
    for r in range(4):

        @pl.when(n1 + r < nh1 * 4)
        def _(r=r):
            at = pl.multiple_of(512 + (n1 + r) * 64, 64)
            ks[pl.ds(at, 64), 0:D] = jnp.zeros((64, D), BF)
            vs[pl.ds(at, 64), 0:D] = jnp.zeros((64, D), BF)

    for rel in range(4):
        z = zhi if rel < 2 else 1 - zhi
        c = core if rel % 2 == 0 else 1 - core
        for sh in range(4):
            yy = lax.rem(y_me - sh + 4, 4)
            at = pl.multiple_of(base + z * 1024 + yy * 256 + c * 128, 128)
            ks[pl.ds(at, 128), 0:D] = kv_refs[rel][sh, ordinal, :, 0:D]
            ks[pl.ds(at, 128), D:] = jnp.zeros((128, D), BF)
            vs[pl.ds(at, 128), 0:D] = kv_refs[rel][sh, ordinal, :, D:]
    kt[...] = ks[...].T
    vt[...] = vs[...].T
    dkt[...] = jnp.zeros_like(dkt)
    dvt[...] = jnp.zeros_like(dvt)
    lnr = lax.broadcasted_iota(jnp.int32, (ROWS, D), 1)
    lane = lax.broadcasted_iota(jnp.int32, (ROWS, CK), 1)
    tok = lax.broadcasted_iota(jnp.int32, (ROWS, CK), 0) % TB + core * TB
    q_s[:, D:] = jnp.where(lnr == 0, 1.0, 0.0).astype(BF)

    def chunk(i, n):
        return pl.ds(pl.multiple_of(i * CK, CK), n * CK)

    def block(sh, carry):
        b = lax.rem(y_me - sh + 4, 4)
        for s0 in range(4):

            @pl.when(sh == s0)
            def _(s0=s0):
                for h in range(HEADS):
                    q_s[h * TB : (h + 1) * TB, 0:D] = qg_refs[s0][:, h * D : (h + 1) * D]
                    ga_s[h * TB : (h + 1) * TB, 0:D] = qg_refs[s0][:, (HEADS + h) * D : (HEADS + h + 1) * D]

        mx[...] = jnp.full_like(mx, NEG)
        nfull = 2 + nh1 + zhi * 4 + b

        def walk(fn, step):
            groups = nfull // step

            def one(i, carry):
                fn(step * i, step, False)
                return carry

            lax.fori_loop(0, groups, one, 0)
            for r in range(step):

                @pl.when(nfull - groups * step == r)
                def _(r=r):
                    fn(nfull - r, r + 1, True)

        def scores(i, n, diag):
            s = dg(q_s[...], kt[:, chunk(i, n)], 1, 0)
            parts = [s[:, k * CK : (k + 1) * CK] for k in range(n)]
            if diag:
                parts[-1] = jnp.where(lane <= tok, parts[-1], NEG)
            for k in range(n):
                s_s[i + k] = parts[k]
            cols = [p[:, h * D : (h + 1) * D] for p in parts for h in range(2)]
            mx[...] = functools.reduce(jnp.maximum, cols, mx[...])

        walk(scores, STEP1)
        m = jnp.max(mx[...], axis=1, keepdims=True)
        mx[...] = jnp.broadcast_to(m * C2, (ROWS, D))
        o_s[...] = jnp.zeros_like(o_s)

        def weigh(i, n, diag):
            mm = mx[...]
            mm = jnp.concatenate([mm, mm], axis=1)
            ws = [jnp.exp2(s_s[i + k] * C2 - mm).astype(BF) for k in range(n)]
            for k in range(n):
                w_s[i + k] = ws[k]
            o_s[...] += dg(jnp.concatenate(ws, axis=1), vs[chunk(i, n), :], 1, 0)

        walk(weigh, STEP2)
        inv = 1.0 / o_s[:, D:]
        att = (o_s[:, :D] * inv).astype(BF)
        gp = (ga_s[:, 0:D].astype(F32) * inv).astype(BF)
        ga_s[:, 0:D] = gp
        for h in range(HEADS):
            att_ref[sh, :, h * D : (h + 1) * D] = att[h * TB : (h + 1) * TB, :]
        delta = jnp.sum(gp.astype(F32) * att.astype(F32), axis=1, keepdims=True)
        ga_s[:, D:] = at_cols(-delta, ROWS).astype(BF)
        qt_s[...] = q_s[:, 0:D].T
        gt_s[...] = gp.T
        dq_s[...] = jnp.zeros_like(dq_s)

        def back(i, n, diag):
            dp = dg(ga_s[...], vt[:, chunk(i, n)], 1, 0).astype(BF)
            ws = [w_s[i + k] for k in range(n)]
            dss = [ws[k] * dp[:, k * CK : (k + 1) * CK] for k in range(n)]
            dq_s[...] += dg(jnp.concatenate(dss, axis=1), ks[chunk(i, n), 0:D], 1, 0)
            for k in range(n):
                dkt[i + k] += dg(qt_s[...], dss[k], 1, 0)
                dvt[i + k] += dg(gt_s[...], ws[k], 1, 0)

        walk(back, STEP3)
        dqv = (dq_s[...] * SCALE).astype(BF)
        for h in range(HEADS):
            dq_ref[sh, :, h * D : (h + 1) * D] = dqv[h * TB : (h + 1) * TB, :]
        return carry

    lax.fori_loop(0, 4, block, 0)

    for rel in range(4):
        z = zhi if rel < 2 else 1 - zhi
        c = core if rel % 2 == 0 else 1 - core
        for sh in range(4):
            yy = lax.rem(y_me - sh + 4, 4)
            i = 2 + nh1 + z * 4 + yy
            half = pl.ds(pl.multiple_of(c * 128, 128), 128)
            dkv_ref[rel, sh, :, 0:D] = (dkt[i, :, half] * SCALE).T.astype(BF)
            dkv_ref[rel, sh, :, D:] = dvt[i, :, half].T.astype(BF)
    for i in range(4):

        @pl.when(i < 2 + nh1)
        def _(i=i):
            s_s[0, 0:CK, 0:D] = (dkt[i] * SCALE).T
            s_s[0, 0:CK, D:] = dvt[i].T
            s_s[1 + i // 2, (i % 2) * CK : (i % 2 + 1) * CK, :] = s_s[0, 0:CK, :]

    n = jnp.int32(0)
    for f in range(8):
        first = s_s[1, f * 64 : (f + 1) * 64, :]
        second = s_s[2, pl.ds(pl.multiple_of(n * 64, 64), 64), :]
        second = jnp.where(see[f], second, 0.0)
        n = n + see[f].astype(jnp.int32)
        if last:
            first = first + acc_ref[f, 0:64, :]
            second = second + acc_ref[f, 64:128, :]
            hg_ref[f] = jnp.concatenate([first, second], axis=0).T.astype(BF)
        else:
            hg_ref[f, 0:64, :] = first
            hg_ref[f, 64:128, :] = second


def span_call(ordinal, pos, cnt, ids, qgs, kvs, hist, acc=None):
    last = acc is not None
    smem = pl.BlockSpec(memory_space=pltpu.SMEM)
    vmem = pl.BlockSpec(memory_space=pltpu.VMEM)
    extra = (acc,) if last else ()
    hg = jax.ShapeDtypeStruct((8, 2 * D, TB), BF) if last else jax.ShapeDtypeStruct((8, TB, 2 * D), F32)
    return pl.pallas_call(
        functools.partial(span_kernel, ordinal, last),
        out_shape=(
            jax.ShapeDtypeStruct((4, TB, HEADS * D), BF),
            jax.ShapeDtypeStruct((4, TB, HEADS * D), BF),
            jax.ShapeDtypeStruct((4, 4, TB, 2 * D), BF),
            hg,
        ),
        in_specs=[smem] * 3 + [vmem] * (9 + len(extra)),
        out_specs=(vmem,) * 4,
        scratch_shapes=[
            pltpu.VMEM((NROW, 2 * D), BF),
            pltpu.VMEM((NROW, 2 * D), BF),
            pltpu.VMEM((ROWS, 2 * D), BF),
            pltpu.VMEM((ROWS, 2 * D), BF),
            pltpu.VMEM((D, ROWS), BF),
            pltpu.VMEM((D, ROWS), BF),
            pltpu.VMEM((NCH, ROWS, CK), F32),
            pltpu.VMEM((NCH, ROWS, CK), BF),
            pltpu.VMEM((ROWS, D), F32),
            pltpu.VMEM((ROWS, 2 * D), F32),
            pltpu.VMEM((ROWS, D), F32),
            pltpu.VMEM((NCH, D, CK), F32),
            pltpu.VMEM((NCH, D, CK), F32),
            pltpu.VMEM((2 * D, NROW), BF),
            pltpu.VMEM((2 * D, NROW), BF),
        ],
        compiler_params=pltpu.CompilerParams(vmem_limit_bytes=56 * 2**20),
        cost_estimate=pl.CostEstimate(
            flops=int(2.5e10), bytes_accessed=6 * 2**20, transcendentals=0
        ),
    )(pos, cnt, ids, *qgs, *kvs, hist, *extra)


def y_shift(a, sh):
    return lax.ppermute(a, "y", [(i, (i + sh) % 4) for i in range(4)])


def flip(a, axis):
    return lax.ppermute(a, axis, [(0, 1), (1, 0)])


def linear(z, y, c):
    return z * 8 + y * 2 + c


def per_device(queries, span_keys, span_values, cotangent, cache_keys, cache_values, hist_count, span_ids):
    zhi, y_me, core = lax.axis_index("zhi"), lax.axis_index("y"), lax.axis_index("core")
    f_me = lax.axis_index("x") * 2 + lax.axis_index("zlo")
    pos = jnp.stack([zhi, y_me, core, f_me]).astype(jnp.int32)

    def head_cols(a, sh, width):
        target = lax.rem(y_me + sh, 4)
        return lax.dynamic_slice_in_dim(a, target * width, width, axis=a.ndim - 1)

    kv_sent = [
        jnp.concatenate([head_cols(span_keys[0], sh, D), head_cols(span_values[0], sh, D)], axis=-1)
        for sh in range(4)
    ]
    kv_own = jnp.stack([kv_sent[0]] + [y_shift(kv_sent[sh], sh) for sh in (1, 2, 3)])
    cache = jnp.stack([cache_keys.T, cache_values.T])
    parts = []
    for k in range(4):
        perm = []
        for head in range(KVH):
            for piece in range(4):
                src = linear(head // 2, 2 * (head % 2) + piece // 2, piece % 2)
                to = (piece + k) % 4
                perm.append((src, linear(to // 2, head, to % 2)))
        parts.append(lax.ppermute(cache, SP, perm))
    hist = lax.all_gather(jnp.stack(parts), FS, axis=0, tiled=False).reshape(8, 4, 2, 32, TB)

    def qg_of(j):
        sent = [
            jnp.concatenate(
                [head_cols(queries[0, j], sh, HEADS * D), head_cols(cotangent[0, j], sh, HEADS * D)], axis=-1
            )
            for sh in range(4)
        ]
        return [sent[0]] + [y_shift(sent[sh], sh) for sh in (1, 2, 3)]

    qg = [qg_of(0), qg_of(1)]
    kv_core = flip(kv_own, "core")
    kv_z = flip(kv_own, "zhi")
    kv_zc = flip(kv_z, "core")
    kvs = (kv_own, kv_core, kv_z, kv_zc)
    att0, dq0, dkv0, acc = span_call(0, pos, hist_count, span_ids, qg[0], kvs, hist)
    att1, dq1, dkv1, hg = span_call(1, pos, hist_count, span_ids, qg[1], kvs, hist, acc)

    def home(a):
        got = [a[0]] + [y_shift(a[sh], 4 - sh) for sh in (1, 2, 3)]
        return place(got)

    def place(got):
        width = got[0].shape[-1]
        out = jnp.zeros(got[0].shape[:-1] + (4 * width,), got[0].dtype)
        for sh in range(4):
            out = lax.dynamic_update_slice_in_dim(out, got[sh], lax.rem(y_me + sh, 4) * width, axis=out.ndim - 1)
        return out

    def reduce_kv(dkv):
        total = dkv[0].astype(F32)
        total += flip(dkv[1], "core").astype(F32)
        total += flip(dkv[2], "zhi").astype(F32)
        both = [(linear(z, y, c), linear(1 - z, y, 1 - c)) for z in range(2) for y in range(4) for c in range(2)]
        total += lax.ppermute(dkv[3], SP, both).astype(F32)
        return total.astype(BF)

    red = jnp.stack([reduce_kv(dkv0), reduce_kv(dkv1)], axis=1)
    hg_all = lax.all_to_all(hg, FS, split_axis=0, concat_axis=0, tiled=True)
    hsum = jnp.sum(hg_all.astype(F32), axis=0).reshape(2, 4, 32, TB)
    mine = []
    for k in range(4):
        perm = []
        for head in range(KVH):
            for zc in range(4):
                piece = (zc + k) % 4
                dst = linear(head // 2, 2 * (head % 2) + piece // 2, piece % 2)
                perm.append((linear(zc // 2, head, zc % 2), dst))
        piece = lax.rem(zhi * 2 + core + k, 4)
        mine.append(lax.ppermute(lax.dynamic_index_in_dim(hsum, piece, 1, keepdims=False), SP, perm))
    hgrad = mine[0] + mine[1] + mine[2] + mine[3]
    attended = jnp.stack([home(att0), home(att1)])[None]
    grad_q = jnp.stack([home(dq0), home(dq1)])[None]
    back = [red[0]] + [y_shift(red[sh], 4 - sh) for sh in (1, 2, 3)]
    grad_k = place([b[..., 0:D] for b in back])[None]
    grad_v = place([b[..., D:] for b in back])[None]
    return attended, grad_q, grad_k, grad_v, hgrad[0].T, hgrad[1].T


def solution(mesh):
    fine = Mesh(mesh.devices.reshape(4, 2, 2, 4, 2), ("x", "zlo", "zhi", "y", "core"))
    tokens = P(FS, None, SP, None)
    resident = P(FS, SP)
    return jax.shard_map(
        per_device,
        mesh=fine,
        in_specs=(tokens,) * 4 + (resident,) * 2 + (P(), P()),
        out_specs=(tokens,) * 4 + (resident,) * 2,
        check_vma=False,
    )
```

time: 443 us -> 256 us (0.58); the launches traced: 436 us -> 253 us
  local copies, waits for them, and re-layouts: 99.4 us -> 9.51 us
  matrix products: 73.5 us -> 0 us
  Pallas kernels: 0 us -> 37.8 us
  blocking collectives: 51.5 us -> 25.2 us
  other arithmetic: 28.6 us -> 5.67 us
  starting transfers between devices: 77 us -> 96.2 us
  between operations: 15.6 us -> 1.25 us
  waiting for transfers between devices: 90.1 us -> 77.5 us
    ppermute x4 -> x41, starting transfers between devices: 10 us -> 89.8 us  [the longest x7 32.8 us: flip(): return lax.ppermute(a, axis, [(0, 1), (1, 0)])]
    dot_general x48 -> x0, matrix products: 73.5 us -> none  [the longest x8 14.7 us: head_pass(): jnp.dot(probability.astype(jnp.bfloat16).T, grad_out, preferred_element_t...]
    ppermute x4 -> x41, waiting for transfers between devices: 6.42 us -> 77.5 us  [the longest x24 55.4 us: y_shift(): return lax.ppermute(a, 'y', [(i, (i + sh) % 4) for i in range(4)])]
    all_to_all x8 -> x1, starting transfers between devices: 66.9 us -> 6.37 us  [per_device(): hg_all = lax.all_to_all(hg, FS, split_axis=0, concat_axis=0, tiled=True)]
    reduce_scatter x2 -> x0, waiting for transfers between devices: 43.8 us -> none  [the longest x1 43.8 us: per_device(): lax.psum_scatter(grad_hist_keys, 'fsdp', scatter_dimension=0, tiled=True)]
    all_to_all x8 -> x1, waiting for transfers between devices: 39.9 us -> 0.01 us  [per_device(): hg_all = lax.all_to_all(hg, FS, split_axis=0, concat_axis=0, tiled=True)]
    pallas_call x0 -> x2, Pallas kernels: none -> 37.8 us  [span_call(): pl.pallas_call(functools.partial(span_kernel, ordinal, last), out_shape=(...]
    another operation x5 -> x4, local copies, waits for them, and re-layouts: 36.6 us -> 0.18 us  [per_device(): attended = jnp.stack([home(att0), home(att1)])[None]]
  transfers between devices with their start and end apart: 14 -> 42, of which waited for: 6 -> 21; matrix products, arithmetic and copies ran while one was open for 22% -> 3% of each run, Pallas kernels for 0% -> 7%
where the time goes in v1:
time: 256 us; the launch traced here: 253 us
  starting transfers between devices  96.2 us (38%)
  waiting for transfers between devices  77.5 us (30%)
  Pallas kernels  37.8 us (15%)
  blocking collectives  25.2 us (10%)
  local copies, waits for them, and re-layouts  9.51 us (4%)
  other arithmetic  5.67 us (2%)
    ppermute x24, waiting for transfers between devices, y_shift(): return lax.ppermute(a, 'y', [(i, (i + sh) % 4) for i in range(4)])  55.4 us
    pallas_call x2, Pallas kernels, span_call(): pl.pallas_call(functools.partial(span_kernel, ordinal, last), out_shape=(...  37.8 us
    ppermute x7, starting transfers between devices, flip(): return lax.ppermute(a, axis, [(0, 1), (1, 0)])  32.8 us
    ppermute x24, starting transfers between devices, y_shift(): return lax.ppermute(a, 'y', [(i, (i + sh) % 4) for i in range(4)])  26.2 us
    all_gather x1, blocking collectives, per_device(): lax.all_gather(jnp.stack(parts), FS, axis=0, tiled=False)  25.2 us
    ppermute x2, starting transfers between devices, reduce_kv(): total += lax.ppermute(dkv[3], SP, both).astype(F32)  12.4 us
    ppermute x7, waiting for transfers between devices, flip(): return lax.ppermute(a, axis, [(0, 1), (1, 0)])  11 us
    ppermute x4, starting transfers between devices, per_device(): parts.append(lax.ppermute(cache, SP, perm))  9.73 us
  transfers between devices with their start and end apart: 42, of which 21 were waited for; matrix products, arithmetic and copies ran while one was open for 3% of the time, Pallas kernels for 7%

profile of v1, /device:TPU:1, one launch (start us, length us, event | category | flops | bytes accessed | tf_op | source)
XLA Modules:
  0.0 253.1 jit_solution(2530304510108499611)
XLA Ops:
  0.6 0.8 pad_maximum_fusion.14
  1.4 0.7 collective-permute-start.9
  2.1 8.6 %collective-permute-start.10 = (bf16[2,32,128]{2,1,0:T(8,128)(2,1)S(1)}, bf16[2,32,128]{2,1,0:T(8,128)(2,1)S(1)}, u32[]{:S(2)}, u32[]{:S(2)}) collective-permute-start(bf16[2,32,128]{2,1,0:T(8,128)(2,1)S(1)} %pad_maximum_fusion.14), channel_id=1, source_target_pairs={{0,1},{1,8},{2,9},{3,0},{4,3},{5,10},{6,11},{7,2},{8,5},{9,12},{10... | collective-permute-start | bytes 49160 | tf_op jit(solution)/shard_map/ppermute | solution.py:300
  10.7 1.1 dynamic-slice_bitcast_fusion.22
  11.9 2.8 %collective-permute-start.4 = (bf16[2,128,256]{2,1,0:T(8,128)(2,1)S(1)}, bf16[2,128,256]{2,1,0:T(8,128)(2,1)S(1)}, u32[]{:S(2)}, u32[]{:S(2)}) collective-permute-start(bf16[2,128,256]{2,1,0:T(8,128)(2,1)S(1)} %pad_maximum_fusion.11), channel_id=1, source_target_pairs={{0,4},{2,6},{4,0},{6,2},{1,5},{3,7},{5,1},{7,3},{8,12},{10,14},{12... | collective-permute-start | bytes 393224 | tf_op jit(solution)/shard_map/ppermute | solution.py:266
  14.8 1.5 collective-permute-start.5
  16.4 1.1 copy-done.3
  17.8 1.1 collective-permute-done.3
  19.4 1.0 collective-permute-done.4
  20.4 1.7 collective-permute-done.5
  22.1 1.9 collective-permute-start.7
  24.0 0.7 pad_maximum_fusion.1.qg0
  25.0 0.8 collective-permute-start.6
  25.7 11.0 %collective-permute-done.7.kv2 = bf16[4,2,128,256]{3,2,1,0:T(8,128)(2,1)S(1)} collective-permute-done((bf16[4,2,128,256]{3,2,1,0:T(8,128)(2,1)S(1)}, bf16[4,2,128,256]{3,2,1,0:T(8,128)(2,1)S(1)}, u32[]{:S(2)}, u32[]{:S(2)}) %collective-permute-start.7) | collective-permute-done | bytes 524320 | tf_op jit(solution)/shard_map/ppermute | solution.py:270
  36.7 1.4 collective-permute-start.8
  38.1 0.7 pad_maximum_fusion.5.qg0
  39.5 0.7 copy-done.11
  40.2 0.7 copy.18.ids_ref
  40.8 2.9 %collective-permute-start = (bf16[128,1024]{1,0:T(8,128)(2,1)S(1)}, bf16[128,1024]{1,0:T(8,128)(2,1)S(1)}, u32[]{:S(2)}, u32[]{:S(2)}) collective-permute-start(bf16[128,1024]{1,0:T(8,128)(2,1)S(1)} %pad_maximum_fusion.2), channel_id=1, source_target_pairs={{0,2},{2,4},{4,6},{6,0},{1,3},{3,5},{5,7},{7,1},{8,10},{10,12},{12... | collective-permute-start | bytes 786440 | tf_op jit(solution)/shard_map/ppermute | solution.py:266
  43.7 1.9 collective-permute-start.1
  46.2 25.2 %all-gather = bf16[32,2,32,128]{3,2,1,0:T(8,128)(2,1)} all-gather(bf16[4,2,32,128]{3,2,1,0:T(8,128)(2,1)S(1)} %pad_maximum_fusion.13), channel_id=2, replica_groups=mesh['x'=4,'zlo'=2,'zhi'=2,'y'=4,'core'=2] {'x','zlo'}, dimensions={0}, use_global_device_ids=true | all-gather | bytes 589824 | tf_op jit(solution)/shard_map/all_gather | solution.py:301
  71.4 1.0 collective-permute-start.18
  72.4 2.1 collective-permute-start.17
  74.6 0.7 copy-done.17
  75.2 17.8 %shard_map.127 = (bf16[4,128,512]{2,1,0:T(8,128)(2,1)}, bf16[4,128,512]{2,1,0:T(8,128)(2,1)}, bf16[4,4,128,256]{3,2,1,0:T(8,128)(2,1)}, f32[8,128,256]{2,1,0:T(8,128)}) custom-call(s32[4]{0:T(128)} %pad_add_fusion.pos_ref, s32[8]{0:T(128)} %cnt_ref.3, s32[8,2]{1,0:T(8,128)} %copy.18.ids_ref, bf16[128,1024]{1,0:T(8,128)(2,1)} %pad_maximum_fusion.1.qg0, ...), custom_call_target="tpu_custom_call" | custom-call | flops 24999999488 | bytes 6291456 | tf_op jit(solution)/shard_map/pallas_call | solution.py:231
  93.1 0.7 copy-done.14
  93.9 20.1 %shard_map.128 = (bf16[4,128,512]{2,1,0:T(8,128)(2,1)}, bf16[4,128,512]{2,1,0:T(8,128)(2,1)}, bf16[4,4,128,256]{3,2,1,0:T(8,128)(2,1)}, bf16[8,256,128]{2,1,0:T(8,128)(2,1)}) custom-call(s32[4]{0:T(128)} %pad_add_fusion.pos_ref, s32[8]{0:T(128)} %cnt_ref.3, s32[8,2]{1,0:T(8,128)} %copy.18.ids_ref, bf16[128,1024]{1,0:T(8,128)(2,1)} %pad_maximum_fusion.5.qg0, ...), custom_call_target="tpu_custom_call" | custom-call | flops 24999999488 | bytes 6291456 | tf_op jit(solution)/shard_map/pallas_call | solution.py:231
  114.0 6.4 %all-to-all-start = ((bf16[8,256,128]{2,1,0:T(8,128)(2,1)}), bf16[8,256,128]{2,1,0:T(8,128)(2,1)S(1)}, u32[]{:S(2)}, u32[]{:S(2)}) async-start(bf16[8,256,128]{2,1,0:T(8,128)(2,1)} %get-tuple-element.21), calls=%async_computation | async-start | bytes 1048576 | tf_op jit(solution)/shard_map/all_to_all | solution.py:340
  120.4 8.2 %collective-permute-start.28 = (bf16[4,128,256]{2,1,0:T(8,128)(2,1)S(1)}, bf16[4,128,256]{2,1,0:T(8,128)(2,1)S(1)}, u32[]{:S(2)}, u32[]{:S(2)}) collective-permute-start(bf16[4,128,256]{2,1,0:T(8,128)(2,1)S(1)} %get-tuple-element.25), channel_id=1, source_target_pairs={{0,1},{1,0},{2,3},{3,2},{4,5},{5,4},{6,7},{7,6},{8,9},{9,8},{10,11... | collective-permute-start | bytes 786440 | tf_op jit(solution)/shard_map/ppermute | solution.py:270
  128.6 17.0 %collective-permute-start.29 = (bf16[4,128,256]{2,1,0:T(8,128)(2,1)S(1)}, bf16[4,128,256]{2,1,0:T(8,128)(2,1)S(1)}, u32[]{:S(2)}, u32[]{:S(2)}) collective-permute-start(bf16[4,128,256]{2,1,0:T(8,128)(2,1)S(1)} %get-tuple-element.27), channel_id=1, source_target_pairs={{0,8},{8,0},{1,9},{9,1},{2,10},{10,2},{3,11},{11,3},{4,12},{12,4},... | collective-permute-start | bytes 786440 | tf_op jit(solution)/shard_map/ppermute | solution.py:270
  146.8 2.4 collective-permute-start.22
  149.3 1.0 copy-done.5
  150.4 1.0 copy-done.6
  151.7 2.0 collective-permute-start.23
  153.7 3.6 %collective-permute-done.23 = bf16[128,512]{1,0:T(8,128)(2,1)S(1)} collective-permute-done((bf16[128,512]{1,0:T(8,128)(2,1)S(1)}, bf16[128,512]{1,0:T(8,128)(2,1)S(1)}, u32[]{:S(2)}, u32[]{:S(2)}) %collective-permute-start.23) | collective-permute-done | bytes 131104 | tf_op jit(solution)/shard_map/ppermute | solution.py:266
  157.3 1.0 collective-permute-start.24
  158.3 4.7 %collective-permute-done.24 = bf16[128,512]{1,0:T(8,128)(2,1)S(1)} collective-permute-done((bf16[128,512]{1,0:T(8,128)(2,1)S(1)}, bf16[128,512]{1,0:T(8,128)(2,1)S(1)}, u32[]{:S(2)}, u32[]{:S(2)}) %collective-permute-start.24) | collective-permute-done | bytes 131104 | tf_op jit(solution)/shard_map/ppermute | solution.py:266
  163.1 1.5 collective-permute-start.25
  164.5 2.3 collective-permute-done.25
  166.9 1.2 collective-permute-start.26
  168.1 4.1 %collective-permute-done.26 = bf16[128,512]{1,0:T(8,128)(2,1)S(1)} collective-permute-done((bf16[128,512]{1,0:T(8,128)(2,1)S(1)}, bf16[128,512]{1,0:T(8,128)(2,1)S(1)}, u32[]{:S(2)}, u32[]{:S(2)}) %collective-permute-start.26) | collective-permute-done | bytes 131104 | tf_op jit(solution)/shard_map/ppermute | solution.py:266
  172.5 5.6 %collective-permute-done.27 = bf16[128,512]{1,0:T(8,128)(2,1)S(1)} collective-permute-done((bf16[128,512]{1,0:T(8,128)(2,1)S(1)}, bf16[128,512]{1,0:T(8,128)(2,1)S(1)}, u32[]{:S(2)}, u32[]{:S(2)}) %collective-permute-start.27) | collective-permute-done | bytes 131104 | tf_op jit(solution)/shard_map/ppermute | solution.py:266
  178.1 0.9 collective-permute-start.13
  179.0 1.1 maximum_bitcast_fusion.1
  180.1 2.2 collective-permute-done.13
  182.5 5.0 %collective-permute-done.14 = bf16[128,512]{1,0:T(8,128)(2,1)S(1)} collective-permute-done((bf16[128,512]{1,0:T(8,128)(2,1)S(1)}, bf16[128,512]{1,0:T(8,128)(2,1)S(1)}, u32[]{:S(2)}, u32[]{:S(2)}) %collective-permute-start.14) | collective-permute-done | bytes 131104 | tf_op jit(solution)/shard_map/ppermute | solution.py:266
  187.6 5.0 %collective-permute-done.15 = bf16[128,512]{1,0:T(8,128)(2,1)S(1)} collective-permute-done((bf16[128,512]{1,0:T(8,128)(2,1)S(1)}, bf16[128,512]{1,0:T(8,128)(2,1)S(1)}, u32[]{:S(2)}, u32[]{:S(2)}) %collective-permute-start.15) | collective-permute-done | bytes 131104 | tf_op jit(solution)/shard_map/ppermute | solution.py:266
  192.6 1.0 collective-permute-start.19
  193.6 2.9 %collective-permute-done.19 = bf16[128,512]{1,0:T(8,128)(2,1)S(1)} collective-permute-done((bf16[128,512]{1,0:T(8,128)(2,1)S(1)}, bf16[128,512]{1,0:T(8,128)(2,1)S(1)}, u32[]{:S(2)}, u32[]{:S(2)}) %collective-permute-start.19) | collective-permute-done | bytes 131104 | tf_op jit(solution)/shard_map/ppermute | solution.py:266
  196.5 0.6 collective-permute-start.20
  197.1 5.8 %collective-permute-done.20 = bf16[128,512]{1,0:T(8,128)(2,1)S(1)} collective-permute-done((bf16[128,512]{1,0:T(8,128)(2,1)S(1)}, bf16[128,512]{1,0:T(8,128)(2,1)S(1)}, u32[]{:S(2)}, u32[]{:S(2)}) %collective-permute-start.20) | collective-permute-done | bytes 131104 | tf_op jit(solution)/shard_map/ppermute | solution.py:266
  202.9 5.0 %collective-permute-done.21 = bf16[128,512]{1,0:T(8,128)(2,1)S(1)} collective-permute-done((bf16[128,512]{1,0:T(8,128)(2,1)S(1)}, bf16[128,512]{1,0:T(8,128)(2,1)S(1)}, u32[]{:S(2)}, u32[]{:S(2)}) %collective-permute-start.21) | collective-permute-done | bytes 131104 | tf_op jit(solution)/shard_map/ppermute | solution.py:266
  207.9 3.1 %collective-permute-start.32 = (bf16[4,128,256]{2,1,0:T(8,128)(2,1)S(1)}, bf16[4,128,256]{2,1,0:T(8,128)(2,1)S(1)}, u32[]{:S(2)}, u32[]{:S(2)}) collective-permute-start(bf16[4,128,256]{2,1,0:T(8,128)(2,1)S(1)} %get-tuple-element.24), channel_id=1, source_target_pairs={{0,8},{8,0},{1,9},{9,1},{2,10},{10,2},{3,11},{11,3},{4,12},{12,4},... | collective-permute-start | bytes 786440 | tf_op jit(solution)/shard_map/ppermute | solution.py:270
  211.1 12.4 %collective-permute-start.33 = (bf16[4,128,256]{2,1,0:T(8,128)(2,1)S(1)}, bf16[4,128,256]{2,1,0:T(8,128)(2,1)S(1)}, u32[]{:S(2)}, u32[]{:S(2)}) collective-permute-start(bf16[4,128,256]{2,1,0:T(8,128)(2,1)S(1)} %get-tuple-element.23), channel_id=1, source_target_pairs={{0,9},{1,8},{2,11},{3,10},{4,13},{5,12},{6,15},{7,14},{8,1},{9,0},... | collective-permute-start | bytes 786440 | tf_op jit(solution)/shard_map/ppermute | solution.py:336
  223.5 1.1 maximum_bitcast_fusion
  224.7 8.5 %collective-permute-done.33 = bf16[4,128,256]{2,1,0:T(8,128)(2,1)S(1)} collective-permute-done((bf16[4,128,256]{2,1,0:T(8,128)(2,1)S(1)}, bf16[4,128,256]{2,1,0:T(8,128)(2,1)S(1)}, u32[]{:S(2)}, u32[]{:S(2)}) %collective-permute-start.33) | collective-permute-done | bytes 262176 | tf_op jit(solution)/shard_map/ppermute | solution.py:336
  233.4 1.6 collective-permute-start.34
  235.8 2.3 collective-permute-done.34
  238.1 2.8 %collective-permute-done.35 = bf16[2,128,256]{2,1,0:T(8,128)(2,1)S(1)} collective-permute-done((bf16[2,128,256]{2,1,0:T(8,128)(2,1)S(1)}, bf16[2,128,256]{2,1,0:T(8,128)(2,1)S(1)}, u32[]{:S(2)}, u32[]{:S(2)}) %collective-permute-start.35) | collective-permute-done | bytes 131104 | tf_op jit(solution)/shard_map/ppermute | solution.py:266
  241.1 0.7 collective-permute-start.37
  241.8 3.8 %collective-permute-start.38 = (f32[2,32,128]{2,1,0:T(8,128)S(1)}, f32[2,32,128]{2,1,0:T(8,128)S(1)}, u32[]{:S(2)}, u32[]{:S(2)}) collective-permute-start(f32[2,32,128]{2,1,0:T(8,128)S(1)} %get-tuple-element.76), channel_id=1, source_target_pairs={{0,1},{1,2},{8,3},{9,0},{2,5},{3,6},{10,7},{11,4},{4,9},{5,10},{12... | collective-permute-start | bytes 98312 | tf_op jit(solution)/shard_map/ppermute | solution.py:351
  245.6 2.0 collective-permute-start.39
  247.6 2.2 collective-permute-start.40
  250.1 2.4 collective-permute-done.40
  (121 shorter events, 7.3 us)
Async XLA Ops:
  0.6 15.6 %copy-start.2 = (bf16[1,2,128,2048]{3,2,1,0:T(8,128)(2,1)S(1)}, bf16[1,2,128,2048]{3,2,1,0:T(8,128)(2,1)}, u32[]{:S(2)}) copy-start(bf16[1,2,128,2048]{3,2,1,0:T(8,128)(2,1)} %param.8) | copy-start | bytes 3145732
  1.4 37.3 %collective-permute-start.9 = (bf16[2,32,128]{2,1,0:T(8,128)(2,1)S(1)}, bf16[2,32,128]{2,1,0:T(8,128)(2,1)S(1)}, u32[]{:S(2)}, u32[]{:S(2)}) collective-permute-start(bf16[2,32,128]{2,1,0:T(8,128)(2,1)S(1)} %pad_maximum_fusion.14), channel_id=1, source_target_pairs={{0,0},{1,1},{2,8},{3,9},{4,2},{5,3},{6,10},{7,11},{8,4},{9,5},{10,... | collective-permute-start | bytes 49160 | tf_op jit(solution)/shard_map/ppermute | solution.py:300
  2.1 38.7 %collective-permute-start.10 = (bf16[2,32,128]{2,1,0:T(8,128)(2,1)S(1)}, bf16[2,32,128]{2,1,0:T(8,128)(2,1)S(1)}, u32[]{:S(2)}, u32[]{:S(2)}) collective-permute-start(bf16[2,32,128]{2,1,0:T(8,128)(2,1)S(1)} %pad_maximum_fusion.14), channel_id=1, source_target_pairs={{0,1},{1,8},{2,9},{3,0},{4,3},{5,10},{6,11},{7,2},{8,5},{9,12},{10... | collective-permute-start | bytes 49160 | tf_op jit(solution)/shard_map/ppermute | solution.py:300
  11.8 7.1 %collective-permute-start.3 = (bf16[2,128,256]{2,1,0:T(8,128)(2,1)S(1)}, bf16[2,128,256]{2,1,0:T(8,128)(2,1)S(1)}, u32[]{:S(2)}, u32[]{:S(2)}) collective-permute-start(bf16[2,128,256]{2,1,0:T(8,128)(2,1)S(1)} %pad_maximum_fusion.10), channel_id=1, source_target_pairs={{0,2},{2,4},{4,6},{6,0},{1,3},{3,5},{5,7},{7,1},{8,10},{10,12},{12... | collective-permute-start | bytes 393224 | tf_op jit(solution)/shard_map/ppermute | solution.py:266
  11.9 8.4 %collective-permute-start.4 = (bf16[2,128,256]{2,1,0:T(8,128)(2,1)S(1)}, bf16[2,128,256]{2,1,0:T(8,128)(2,1)S(1)}, u32[]{:S(2)}, u32[]{:S(2)}) collective-permute-start(bf16[2,128,256]{2,1,0:T(8,128)(2,1)S(1)} %pad_maximum_fusion.11), channel_id=1, source_target_pairs={{0,4},{2,6},{4,0},{6,2},{1,5},{3,7},{5,1},{7,3},{8,12},{10,14},{12... | collective-permute-start | bytes 393224 | tf_op jit(solution)/shard_map/ppermute | solution.py:266
  14.8 7.3 %collective-permute-start.5 = (bf16[2,128,256]{2,1,0:T(8,128)(2,1)S(1)}, bf16[2,128,256]{2,1,0:T(8,128)(2,1)S(1)}, u32[]{:S(2)}, u32[]{:S(2)}) collective-permute-start(bf16[2,128,256]{2,1,0:T(8,128)(2,1)S(1)} %pad_maximum_fusion.12), channel_id=1, source_target_pairs={{0,6},{2,0},{4,2},{6,4},{1,7},{3,1},{5,3},{7,5},{8,14},{10,8},{12,... | collective-permute-start | bytes 393224 | tf_op jit(solution)/shard_map/ppermute | solution.py:266
  16.3 1.2 copy-start.3
  18.9 24.8 %collective-permute-start.11 = (bf16[2,32,128]{2,1,0:T(8,128)(2,1)S(1)}, bf16[2,32,128]{2,1,0:T(8,128)(2,1)S(1)}, u32[]{:S(2)}, u32[]{:S(2)}) collective-permute-start(bf16[2,32,128]{2,1,0:T(8,128)(2,1)S(1)} %pad_maximum_fusion.14), channel_id=1, source_target_pairs={{0,8},{1,9},{2,0},{3,1},{4,10},{5,11},{6,2},{7,3},{8,12},{9,13},{1... | collective-permute-start | bytes 49160 | tf_op jit(solution)/shard_map/ppermute | solution.py:300
  22.1 2.8 %copy-start.4 = (bf16[4,2,128,256]{3,2,1,0:T(8,128)(2,1)}, bf16[4,2,128,256]{3,2,1,0:T(8,128)(2,1)S(1)}, u32[]{:S(2)}) copy-start(bf16[4,2,128,256]{3,2,1,0:T(8,128)(2,1)S(1)} %pad_maximum_fusion.kv0) | copy-start | bytes 1572868
  22.1 14.6 %collective-permute-start.7 = (bf16[4,2,128,256]{3,2,1,0:T(8,128)(2,1)S(1)}, bf16[4,2,128,256]{3,2,1,0:T(8,128)(2,1)S(1)}, u32[]{:S(2)}, u32[]{:S(2)}) collective-permute-start(bf16[4,2,128,256]{3,2,1,0:T(8,128)(2,1)S(1)} %pad_maximum_fusion.kv0), channel_id=1, source_target_pairs={{0,8},{8,0},{1,9},{9,1},{2,10},{10,2},{3,11},{11,3},{4,12},{12,4},... | collective-permute-start | bytes 1572872 | tf_op jit(solution)/shard_map/ppermute | solution.py:270
  25.0 49.6 %collective-permute-start.6 = (bf16[4,2,128,256]{3,2,1,0:T(8,128)(2,1)S(1)}, bf16[4,2,128,256]{3,2,1,0:T(8,128)(2,1)}, u32[]{:S(2)}, u32[]{:S(2)}) collective-permute-start(bf16[4,2,128,256]{3,2,1,0:T(8,128)(2,1)S(1)} %pad_maximum_fusion.kv0), channel_id=1, source_target_pairs={{0,1},{1,0},{2,3},{3,2},{4,5},{5,4},{6,7},{7,6},{8,9},{9,8},{10,11... | collective-permute-start | bytes 1572872 | tf_op jit(solution)/shard_map/ppermute | solution.py:270
  36.7 34.7 %copy-start.12 = (bf16[4,2,128,256]{3,2,1,0:T(8,128)(2,1)}, bf16[4,2,128,256]{3,2,1,0:T(8,128)(2,1)S(1)}, u32[]{:S(2)}) copy-start(bf16[4,2,128,256]{3,2,1,0:T(8,128)(2,1)S(1)} %collective-permute-done.7.kv2) | copy-start | bytes 1572868
  36.7 37.8 %collective-permute-start.8 = (bf16[4,2,128,256]{3,2,1,0:T(8,128)(2,1)S(1)}, bf16[4,2,128,256]{3,2,1,0:T(8,128)(2,1)}, u32[]{:S(2)}, u32[]{:S(2)}) collective-permute-start(bf16[4,2,128,256]{3,2,1,0:T(8,128)(2,1)S(1)} %collective-permute-done.7.kv2), channel_id=1, source_target_pairs={{0,1},{1,0},{2,3},{3,2},{4,5},{5,4},{6,7},{7,6},{8,9},{9,8},{10,11... | collective-permute-start | bytes 1572872 | tf_op jit(solution)/shard_map/ppermute | solution.py:270
  38.8 6.8 %collective-permute-start.12 = (bf16[2,32,128]{2,1,0:T(8,128)(2,1)S(1)}, bf16[2,32,128]{2,1,0:T(8,128)(2,1)S(1)}, u32[]{:S(2)}, u32[]{:S(2)}) collective-permute-start(bf16[2,32,128]{2,1,0:T(8,128)(2,1)S(1)} %pad_maximum_fusion.14), channel_id=1, source_target_pairs={{0,9},{1,0},{2,1},{3,8},{4,11},{5,2},{6,3},{7,10},{8,13},{9,4},{10... | collective-permute-start | bytes 49160 | tf_op jit(solution)/shard_map/ppermute | solution.py:300
  39.5 0.7 copy-start.11
  40.8 30.6 %collective-permute-start = (bf16[128,1024]{1,0:T(8,128)(2,1)S(1)}, bf16[128,1024]{1,0:T(8,128)(2,1)S(1)}, u32[]{:S(2)}, u32[]{:S(2)}) collective-permute-start(bf16[128,1024]{1,0:T(8,128)(2,1)S(1)} %pad_maximum_fusion.2), channel_id=1, source_target_pairs={{0,2},{2,4},{4,6},{6,0},{1,3},{3,5},{5,7},{7,1},{8,10},{10,12},{12... | collective-permute-start | bytes 786440 | tf_op jit(solution)/shard_map/ppermute | solution.py:266
  43.7 28.7 %collective-permute-start.1 = (bf16[128,1024]{1,0:T(8,128)(2,1)S(1)}, bf16[128,1024]{1,0:T(8,128)(2,1)S(1)}, u32[]{:S(2)}, u32[]{:S(2)}) collective-permute-start(bf16[128,1024]{1,0:T(8,128)(2,1)S(1)} %pad_maximum_fusion.3), channel_id=1, source_target_pairs={{0,4},{2,6},{4,0},{6,2},{1,5},{3,7},{5,1},{7,3},{8,12},{10,14},{12... | collective-permute-start | bytes 786440 | tf_op jit(solution)/shard_map/ppermute | solution.py:266
  45.6 28.9 %collective-permute-start.2 = (bf16[128,1024]{1,0:T(8,128)(2,1)S(1)}, bf16[128,1024]{1,0:T(8,128)(2,1)S(1)}, u32[]{:S(2)}, u32[]{:S(2)}) collective-permute-start(bf16[128,1024]{1,0:T(8,128)(2,1)S(1)} %pad_maximum_fusion.4), channel_id=1, source_target_pairs={{0,6},{2,0},{4,2},{6,4},{1,7},{3,1},{5,3},{7,5},{8,14},{10,8},{12,... | collective-permute-start | bytes 786440 | tf_op jit(solution)/shard_map/ppermute | solution.py:266
  71.4 3.2 %copy-start.13 = (bf16[128,1024]{1,0:T(8,128)(2,1)}, bf16[128,1024]{1,0:T(8,128)(2,1)S(1)}, u32[]{:S(2)}) copy-start(bf16[128,1024]{1,0:T(8,128)(2,1)S(1)} %collective-permute-done.qg1) | copy-start | bytes 786436
  71.4 21.6 %collective-permute-start.18 = (bf16[128,1024]{1,0:T(8,128)(2,1)S(1)}, bf16[128,1024]{1,0:T(8,128)(2,1)S(1)}, u32[]{:S(2)}, u32[]{:S(2)}) collective-permute-start(bf16[128,1024]{1,0:T(8,128)(2,1)S(1)} %pad_maximum_fusion.8), channel_id=1, source_target_pairs={{0,6},{2,0},{4,2},{6,4},{1,7},{3,1},{5,3},{7,5},{8,14},{10,8},{12,... | collective-permute-start | bytes 786440 | tf_op jit(solution)/shard_map/ppermute | solution.py:266
  72.4 2.2 copy-start.15
  72.4 20.6 %collective-permute-start.17 = (bf16[128,1024]{1,0:T(8,128)(2,1)S(1)}, bf16[128,1024]{1,0:T(8,128)(2,1)S(1)}, u32[]{:S(2)}, u32[]{:S(2)}) collective-permute-start(bf16[128,1024]{1,0:T(8,128)(2,1)S(1)} %pad_maximum_fusion.7), channel_id=1, source_target_pairs={{0,4},{2,6},{4,0},{6,2},{1,5},{3,7},{5,1},{7,3},{8,12},{10,14},{12... | collective-permute-start | bytes 786440 | tf_op jit(solution)/shard_map/ppermute | solution.py:266
  74.5 0.7 copy-start.17
  74.5 18.5 %collective-permute-start.16 = (bf16[128,1024]{1,0:T(8,128)(2,1)S(1)}, bf16[128,1024]{1,0:T(8,128)(2,1)S(1)}, u32[]{:S(2)}, u32[]{:S(2)}) collective-permute-start(bf16[128,1024]{1,0:T(8,128)(2,1)S(1)} %pad_maximum_fusion.6), channel_id=1, source_target_pairs={{0,2},{2,4},{4,6},{6,0},{1,3},{3,5},{5,7},{7,1},{8,10},{10,12},{12... | collective-permute-start | bytes 786440 | tf_op jit(solution)/shard_map/ppermute | solution.py:266
  93.0 0.7 copy-start.14
  93.0 0.8 copy-start.16
  93.1 0.8 copy-start.18
  113.9 6.4 %copy-start = (bf16[4,4,128,256]{3,2,1,0:T(8,128)(2,1)S(1)}, bf16[4,4,128,256]{3,2,1,0:T(8,128)(2,1)}, u32[]{:S(2)}) copy-start(bf16[4,4,128,256]{3,2,1,0:T(8,128)(2,1)} %get-tuple-element.19) | copy-start | bytes 3145732
  114.0 127.0 %all-to-all-start = ((bf16[8,256,128]{2,1,0:T(8,128)(2,1)}), bf16[8,256,128]{2,1,0:T(8,128)(2,1)S(1)}, u32[]{:S(2)}, u32[]{:S(2)}) async-start(bf16[8,256,128]{2,1,0:T(8,128)(2,1)} %get-tuple-element.21), calls=%async_computation | async-start | bytes 1048576 | tf_op jit(solution)/shard_map/all_to_all | solution.py:340
  120.3 25.3 %copy-start.1 = (bf16[4,4,128,256]{3,2,1,0:T(8,128)(2,1)S(1)}, bf16[4,4,128,256]{3,2,1,0:T(8,128)(2,1)}, u32[]{:S(2)}) copy-start(bf16[4,4,128,256]{3,2,1,0:T(8,128)(2,1)} %get-tuple-element.20) | copy-start | bytes 3145732
  120.4 90.7 %collective-permute-start.28 = (bf16[4,128,256]{2,1,0:T(8,128)(2,1)S(1)}, bf16[4,128,256]{2,1,0:T(8,128)(2,1)S(1)}, u32[]{:S(2)}, u32[]{:S(2)}) collective-permute-start(bf16[4,128,256]{2,1,0:T(8,128)(2,1)S(1)} %get-tuple-element.25), channel_id=1, source_target_pairs={{0,1},{1,0},{2,3},{3,2},{4,5},{5,4},{6,7},{7,6},{8,9},{9,8},{10,11... | collective-permute-start | bytes 786440 | tf_op jit(solution)/shard_map/ppermute | solution.py:270
  128.6 95.9 %collective-permute-start.29 = (bf16[4,128,256]{2,1,0:T(8,128)(2,1)S(1)}, bf16[4,128,256]{2,1,0:T(8,128)(2,1)S(1)}, u32[]{:S(2)}, u32[]{:S(2)}) collective-permute-start(bf16[4,128,256]{2,1,0:T(8,128)(2,1)S(1)} %get-tuple-element.27), channel_id=1, source_target_pairs={{0,8},{8,0},{1,9},{9,1},{2,10},{10,2},{3,11},{11,3},{4,12},{12,4},... | collective-permute-start | bytes 786440 | tf_op jit(solution)/shard_map/ppermute | solution.py:270
  145.6 78.9 %collective-permute-start.30 = (bf16[4,128,256]{2,1,0:T(8,128)(2,1)S(1)}, bf16[4,128,256]{2,1,0:T(8,128)(2,1)S(1)}, u32[]{:S(2)}, u32[]{:S(2)}) collective-permute-start(bf16[4,128,256]{2,1,0:T(8,128)(2,1)S(1)} %get-tuple-element.26), channel_id=1, source_target_pairs={{0,9},{1,8},{2,11},{3,10},{4,13},{5,12},{6,15},{7,14},{8,1},{9,0},... | collective-permute-start | bytes 786440 | tf_op jit(solution)/shard_map/ppermute | solution.py:336
  145.7 1.0 copy-start.7
  145.7 79.0 %collective-permute-start.31 = (bf16[4,128,256]{2,1,0:T(8,128)(2,1)S(1)}, bf16[4,128,256]{2,1,0:T(8,128)(2,1)S(1)}, u32[]{:S(2)}, u32[]{:S(2)}) collective-permute-start(bf16[4,128,256]{2,1,0:T(8,128)(2,1)S(1)} %get-tuple-element.22), channel_id=1, source_target_pairs={{0,1},{1,0},{2,3},{3,2},{4,5},{5,4},{6,7},{7,6},{8,9},{9,8},{10,11... | collective-permute-start | bytes 786440 | tf_op jit(solution)/shard_map/ppermute | solution.py:270
  146.8 2.4 copy-start.8
  146.8 4.9 %collective-permute-start.22 = (bf16[128,512]{1,0:T(8,128)(2,1)S(1)}, bf16[128,512]{1,0:T(8,128)(2,1)S(1)}, u32[]{:S(2)}, u32[]{:S(2)}) collective-permute-start(bf16[128,512]{1,0:T(8,128)(2,1)S(1)} %get-tuple-element.38), channel_id=1, source_target_pairs={{0,6},{2,0},{4,2},{6,4},{1,7},{3,1},{5,3},{7,5},{8,14},{10,8},{12,... | collective-permute-start | bytes 393224 | tf_op jit(solution)/shard_map/ppermute | solution.py:266
  149.3 1.0 copy-start.5
  150.3 1.0 copy-start.6
  151.7 5.6 %collective-permute-start.23 = (bf16[128,512]{1,0:T(8,128)(2,1)S(1)}, bf16[128,512]{1,0:T(8,128)(2,1)S(1)}, u32[]{:S(2)}, u32[]{:S(2)}) collective-permute-start(bf16[128,512]{1,0:T(8,128)(2,1)S(1)} %get-tuple-element.37), channel_id=1, source_target_pairs={{0,4},{2,6},{4,0},{6,2},{1,5},{3,7},{5,1},{7,3},{8,12},{10,14},{12... | collective-permute-start | bytes 393224 | tf_op jit(solution)/shard_map/ppermute | solution.py:266
  157.3 5.8 %collective-permute-start.24 = (bf16[128,512]{1,0:T(8,128)(2,1)S(1)}, bf16[128,512]{1,0:T(8,128)(2,1)S(1)}, u32[]{:S(2)}, u32[]{:S(2)}) collective-permute-start(bf16[128,512]{1,0:T(8,128)(2,1)S(1)} %get-tuple-element.36), channel_id=1, source_target_pairs={{0,2},{2,4},{4,6},{6,0},{1,3},{3,5},{5,7},{7,1},{8,10},{10,12},{12... | collective-permute-start | bytes 393224 | tf_op jit(solution)/shard_map/ppermute | solution.py:266
  163.1 3.8 %collective-permute-start.25 = (bf16[128,512]{1,0:T(8,128)(2,1)S(1)}, bf16[128,512]{1,0:T(8,128)(2,1)S(1)}, u32[]{:S(2)}, u32[]{:S(2)}) collective-permute-start(bf16[128,512]{1,0:T(8,128)(2,1)S(1)} %get-tuple-element.42), channel_id=1, source_target_pairs={{0,6},{2,0},{4,2},{6,4},{1,7},{3,1},{5,3},{7,5},{8,14},{10,8},{12,... | collective-permute-start | bytes 393224 | tf_op jit(solution)/shard_map/ppermute | solution.py:266
  166.9 5.3 %collective-permute-start.26 = (bf16[128,512]{1,0:T(8,128)(2,1)S(1)}, bf16[128,512]{1,0:T(8,128)(2,1)S(1)}, u32[]{:S(2)}, u32[]{:S(2)}) collective-permute-start(bf16[128,512]{1,0:T(8,128)(2,1)S(1)} %get-tuple-element.41), channel_id=1, source_target_pairs={{0,4},{2,6},{4,0},{6,2},{1,5},{3,7},{5,1},{7,3},{8,12},{10,14},{12... | collective-permute-start | bytes 393224 | tf_op jit(solution)/shard_map/ppermute | solution.py:266
  172.2 5.9 %collective-permute-start.27 = (bf16[128,512]{1,0:T(8,128)(2,1)S(1)}, bf16[128,512]{1,0:T(8,128)(2,1)S(1)}, u32[]{:S(2)}, u32[]{:S(2)}) collective-permute-start(bf16[128,512]{1,0:T(8,128)(2,1)S(1)} %get-tuple-element.40), channel_id=1, source_target_pairs={{0,2},{2,4},{4,6},{6,0},{1,3},{3,5},{5,7},{7,1},{8,10},{10,12},{12... | collective-permute-start | bytes 393224 | tf_op jit(solution)/shard_map/ppermute | solution.py:266
  178.1 4.1 %collective-permute-start.13 = (bf16[128,512]{1,0:T(8,128)(2,1)S(1)}, bf16[128,512]{1,0:T(8,128)(2,1)S(1)}, u32[]{:S(2)}, u32[]{:S(2)}) collective-permute-start(bf16[128,512]{1,0:T(8,128)(2,1)S(1)} %get-tuple-element.46), channel_id=1, source_target_pairs={{0,6},{2,0},{4,2},{6,4},{1,7},{3,1},{5,3},{7,5},{8,14},{10,8},{12,... | collective-permute-start | bytes 393224 | tf_op jit(solution)/shard_map/ppermute | solution.py:266
  182.2 5.3 %collective-permute-start.14 = (bf16[128,512]{1,0:T(8,128)(2,1)S(1)}, bf16[128,512]{1,0:T(8,128)(2,1)S(1)}, u32[]{:S(2)}, u32[]{:S(2)}) collective-permute-start(bf16[128,512]{1,0:T(8,128)(2,1)S(1)} %get-tuple-element.45), channel_id=1, source_target_pairs={{0,4},{2,6},{4,0},{6,2},{1,5},{3,7},{5,1},{7,3},{8,12},{10,14},{12... | collective-permute-start | bytes 393224 | tf_op jit(solution)/shard_map/ppermute | solution.py:266
  187.6 5.0 %collective-permute-start.15 = (bf16[128,512]{1,0:T(8,128)(2,1)S(1)}, bf16[128,512]{1,0:T(8,128)(2,1)S(1)}, u32[]{:S(2)}, u32[]{:S(2)}) collective-permute-start(bf16[128,512]{1,0:T(8,128)(2,1)S(1)} %get-tuple-element.44), channel_id=1, source_target_pairs={{0,2},{2,4},{4,6},{6,0},{1,3},{3,5},{5,7},{7,1},{8,10},{10,12},{12... | collective-permute-start | bytes 393224 | tf_op jit(solution)/shard_map/ppermute | solution.py:266
  192.6 3.9 %collective-permute-start.19 = (bf16[128,512]{1,0:T(8,128)(2,1)S(1)}, bf16[128,512]{1,0:T(8,128)(2,1)S(1)}, u32[]{:S(2)}, u32[]{:S(2)}) collective-permute-start(bf16[128,512]{1,0:T(8,128)(2,1)S(1)} %get-tuple-element.50), channel_id=1, source_target_pairs={{0,6},{2,0},{4,2},{6,4},{1,7},{3,1},{5,3},{7,5},{8,14},{10,8},{12,... | collective-permute-start | bytes 393224 | tf_op jit(solution)/shard_map/ppermute | solution.py:266
  196.5 6.4 %collective-permute-start.20 = (bf16[128,512]{1,0:T(8,128)(2,1)S(1)}, bf16[128,512]{1,0:T(8,128)(2,1)S(1)}, u32[]{:S(2)}, u32[]{:S(2)}) collective-permute-start(bf16[128,512]{1,0:T(8,128)(2,1)S(1)} %get-tuple-element.49), channel_id=1, source_target_pairs={{0,4},{2,6},{4,0},{6,2},{1,5},{3,7},{5,1},{7,3},{8,12},{10,14},{12... | collective-permute-start | bytes 393224 | tf_op jit(solution)/shard_map/ppermute | solution.py:266
  202.9 5.0 %collective-permute-start.21 = (bf16[128,512]{1,0:T(8,128)(2,1)S(1)}, bf16[128,512]{1,0:T(8,128)(2,1)S(1)}, u32[]{:S(2)}, u32[]{:S(2)}) collective-permute-start(bf16[128,512]{1,0:T(8,128)(2,1)S(1)} %get-tuple-element.48), channel_id=1, source_target_pairs={{0,2},{2,4},{4,6},{6,0},{1,3},{3,5},{5,7},{7,1},{8,10},{10,12},{12... | collective-permute-start | bytes 393224 | tf_op jit(solution)/shard_map/ppermute | solution.py:266
  207.9 16.7 %collective-permute-start.32 = (bf16[4,128,256]{2,1,0:T(8,128)(2,1)S(1)}, bf16[4,128,256]{2,1,0:T(8,128)(2,1)S(1)}, u32[]{:S(2)}, u32[]{:S(2)}) collective-permute-start(bf16[4,128,256]{2,1,0:T(8,128)(2,1)S(1)} %get-tuple-element.24), channel_id=1, source_target_pairs={{0,8},{8,0},{1,9},{9,1},{2,10},{10,2},{3,11},{11,3},{4,12},{12,4},... | collective-permute-start | bytes 786440 | tf_op jit(solution)/shard_map/ppermute | solution.py:270
  211.1 22.1 %collective-permute-start.33 = (bf16[4,128,256]{2,1,0:T(8,128)(2,1)S(1)}, bf16[4,128,256]{2,1,0:T(8,128)(2,1)S(1)}, u32[]{:S(2)}, u32[]{:S(2)}) collective-permute-start(bf16[4,128,256]{2,1,0:T(8,128)(2,1)S(1)} %get-tuple-element.23), channel_id=1, source_target_pairs={{0,9},{1,8},{2,11},{3,10},{4,13},{5,12},{6,15},{7,14},{8,1},{9,0},... | collective-permute-start | bytes 786440 | tf_op jit(solution)/shard_map/ppermute | solution.py:336
  233.4 4.6 %collective-permute-start.34 = (bf16[2,128,256]{2,1,0:T(8,128)(2,1)S(1)}, bf16[2,128,256]{2,1,0:T(8,128)(2,1)S(1)}, u32[]{:S(2)}, u32[]{:S(2)}) collective-permute-start(bf16[2,128,256]{2,1,0:T(8,128)(2,1)S(1)} %get-tuple-element.34), channel_id=1, source_target_pairs={{0,6},{2,0},{4,2},{6,4},{1,7},{3,1},{5,3},{7,5},{8,14},{10,8},{12,... | collective-permute-start | bytes 393224 | tf_op jit(solution)/shard_map/ppermute | solution.py:266
  235.1 5.8 %collective-permute-start.35 = (bf16[2,128,256]{2,1,0:T(8,128)(2,1)S(1)}, bf16[2,128,256]{2,1,0:T(8,128)(2,1)S(1)}, u32[]{:S(2)}, u32[]{:S(2)}) collective-permute-start(bf16[2,128,256]{2,1,0:T(8,128)(2,1)S(1)} %get-tuple-element.35), channel_id=1, source_target_pairs={{0,4},{2,6},{4,0},{6,2},{1,5},{3,7},{5,1},{7,3},{8,12},{10,14},{12... | collective-permute-start | bytes 393224 | tf_op jit(solution)/shard_map/ppermute | solution.py:266
  235.2 14.6 %collective-permute-start.36 = (bf16[2,128,256]{2,1,0:T(8,128)(2,1)S(1)}, bf16[2,128,256]{2,1,0:T(8,128)(2,1)S(1)}, u32[]{:S(2)}, u32[]{:S(2)}) collective-permute-start(bf16[2,128,256]{2,1,0:T(8,128)(2,1)S(1)} %get-tuple-element.32), channel_id=1, source_target_pairs={{0,2},{2,4},{4,6},{6,0},{1,3},{3,5},{5,7},{7,1},{8,10},{10,12},{12... | collective-permute-start | bytes 393224 | tf_op jit(solution)/shard_map/ppermute | solution.py:266
  241.1 8.8 %collective-permute-start.37 = (f32[2,32,128]{2,1,0:T(8,128)S(1)}, f32[2,32,128]{2,1,0:T(8,128)S(1)}, u32[]{:S(2)}, u32[]{:S(2)}) collective-permute-start(f32[2,32,128]{2,1,0:T(8,128)S(1)} %get-tuple-element.79), channel_id=1, source_target_pairs={{0,0},{1,1},{8,2},{9,3},{2,4},{3,5},{10,6},{11,7},{4,8},{5,9},{12,... | collective-permute-start | bytes 98312 | tf_op jit(solution)/shard_map/ppermute | solution.py:351
  241.8 8.1 %collective-permute-start.38 = (f32[2,32,128]{2,1,0:T(8,128)S(1)}, f32[2,32,128]{2,1,0:T(8,128)S(1)}, u32[]{:S(2)}, u32[]{:S(2)}) collective-permute-start(f32[2,32,128]{2,1,0:T(8,128)S(1)} %get-tuple-element.76), channel_id=1, source_target_pairs={{0,1},{1,2},{8,3},{9,0},{2,5},{3,6},{10,7},{11,4},{4,9},{5,10},{12... | collective-permute-start | bytes 98312 | tf_op jit(solution)/shard_map/ppermute | solution.py:351
  245.6 4.5 %collective-permute-start.39 = (f32[2,32,128]{2,1,0:T(8,128)S(1)}, f32[2,32,128]{2,1,0:T(8,128)S(1)}, u32[]{:S(2)}, u32[]{:S(2)}) collective-permute-start(f32[2,32,128]{2,1,0:T(8,128)S(1)} %get-tuple-element.78), channel_id=1, source_target_pairs={{0,2},{1,3},{8,0},{9,1},{2,6},{3,7},{10,4},{11,5},{4,10},{5,11},{1... | collective-permute-start | bytes 98312 | tf_op jit(solution)/shard_map/ppermute | solution.py:351
  247.6 4.8 %collective-permute-start.40 = (f32[2,32,128]{2,1,0:T(8,128)S(1)}, f32[2,32,128]{2,1,0:T(8,128)S(1)}, u32[]{:S(2)}, u32[]{:S(2)}) collective-permute-start(f32[2,32,128]{2,1,0:T(8,128)S(1)} %get-tuple-element.77), channel_id=1, source_target_pairs={{0,3},{1,0},{8,1},{9,2},{2,7},{3,4},{10,5},{11,6},{4,11},{5,8},{12... | collective-permute-start | bytes 98312 | tf_op jit(solution)/shard_map/ppermute | solution.py:351
  249.8 3.2 %copy-start.9 = (bf16[1,2,128,512]{3,2,1,0:T(8,128)(2,1)}, bf16[1,2,128,512]{3,2,1,0:T(8,128)(2,1)S(1)}, u32[]{:S(2)}) copy-start(bf16[1,2,128,512]{3,2,1,0:T(8,128)(2,1)S(1)} %get-tuple-element.80) | copy-start | bytes 786436
  249.9 3.2 %copy-start.10 = (bf16[1,2,128,512]{3,2,1,0:T(8,128)(2,1)}, bf16[1,2,128,512]{3,2,1,0:T(8,128)(2,1)S(1)}, u32[]{:S(2)}) copy-start(bf16[1,2,128,512]{3,2,1,0:T(8,128)(2,1)S(1)} %get-tuple-element.81) | copy-start | bytes 786436

commit v2 on v1

--- a/solution.py
+++ b/solution.py
@@ -50,13 +50,15 @@
 
 
 def span_kernel(
-    ordinal, last, pos_ref, cnt_ref, ids_ref, qg0, qg1, qg2, qg3, kv0, kv1, kv2, kv3, hist_ref, *rest
+    ordinal, pos_ref, cnt_ref, ids_ref, qg_ref, kv0, kv1, kv2, kv3, h0, h1, *rest
 ):
+    last = ordinal == 1
     if last:
         acc_ref, *rest = rest
-    (att_ref, dq_ref, dkv_ref, hg_ref, ks, vs, q_s, ga_s, qt_s, gt_s, s_s, w_s, mx, o_s, dq_s, dkt, dvt, kt, vt) = rest
-    zhi, y_me, core, f_me = pos_ref[0], pos_ref[1], pos_ref[2], pos_ref[3]
-    qg_refs = (qg0, qg1, qg2, qg3)
+    (out_ref, keep_ref, send_ref, hg_ref, *rest) = rest
+    (ks, vs, q_s, ga_s, qt_s, gt_s, s_s, w_s, mx, o_s, dq_s, dkt, dvt, kt, vt) = rest
+    zhi, y_me, core, x_me, zlo = pos_ref[0], pos_ref[1], pos_ref[2], pos_ref[3], pos_ref[4]
+    f_me = x_me * 2 + zlo
     kv_refs = (kv0, kv1, kv2, kv3)
     span_id = ids_ref[f_me, ordinal]
     see = [(cnt_ref[f] > 1) & (f + 8 < span_id) for f in range(8)]
@@ -69,12 +71,15 @@
     rw = lax.broadcasted_iota(jnp.int32, (HIST, D), 0)
     ks[0:HIST, D:] = jnp.where((ln == 0) & (rw >= 512 + n1 * 64), NEG, 0.0).astype(BF)
     base = pl.multiple_of(512 + nh1 * CK, CK)
-    zc = zhi * 2 + core
     n = jnp.int32(0)
+
+    def history(f, piece, i):
+        c = jnp.where(core == piece % 2, 0, 1)
+        at = (c, lax.rem(x_me - f // 2 + 4, 4), jnp.where(zlo == f % 2, 0, 1), i)
+        return jnp.where(zhi == piece // 2, h0[at], h1[at])
+
     for f in range(8):
-        rows = jnp.concatenate(
-            [hist_ref[f, lax.rem(zc - p + 4, 4), i] for i in range(2) for p in range(4)], axis=0
-        ).T
+        rows = jnp.concatenate([history(f, p, i) for i in range(2) for p in range(4)], axis=0).T
         ks[f * 64 : (f + 1) * 64, 0:D] = rows[0:64, 0:D]
         vs[f * 64 : (f + 1) * 64, 0:D] = rows[0:64, D:]
         at = pl.multiple_of(512 + n * 64, 64)
@@ -110,16 +115,10 @@
     def chunk(i, n):
         return pl.ds(pl.multiple_of(i * CK, CK), n * CK)
 
-    def block(sh, carry):
-        b = lax.rem(y_me - sh + 4, 4)
-        for s0 in range(4):
-
-            @pl.when(sh == s0)
-            def _(s0=s0):
-                for h in range(HEADS):
-                    q_s[h * TB : (h + 1) * TB, 0:D] = qg_refs[s0][:, h * D : (h + 1) * D]
-                    ga_s[h * TB : (h + 1) * TB, 0:D] = qg_refs[s0][:, (HEADS + h) * D : (HEADS + h + 1) * D]
-
+    def block(b, carry):
+        for h in range(HEADS):
+            q_s[h * TB : (h + 1) * TB, 0:D] = qg_ref[b, :, h * D : (h + 1) * D]
+            ga_s[h * TB : (h + 1) * TB, 0:D] = qg_ref[b, :, (HEADS + h) * D : (HEADS + h + 1) * D]
         mx[...] = jnp.full_like(mx, NEG)
         nfull = 2 + nh1 + zhi * 4 + b
 
@@ -166,7 +165,7 @@
         gp = (ga_s[:, 0:D].astype(F32) * inv).astype(BF)
         ga_s[:, 0:D] = gp
         for h in range(HEADS):
-            att_ref[sh, :, h * D : (h + 1) * D] = att[h * TB : (h + 1) * TB, :]
+            out_ref[b, :, h * D : (h + 1) * D] = att[h * TB : (h + 1) * TB, :]
         delta = jnp.sum(gp.astype(F32) * att.astype(F32), axis=1, keepdims=True)
         ga_s[:, D:] = at_cols(-delta, ROWS).astype(BF)
         qt_s[...] = q_s[:, 0:D].T
@@ -185,7 +184,7 @@
         walk(back, STEP3)
         dqv = (dq_s[...] * SCALE).astype(BF)
         for h in range(HEADS):
-            dq_ref[sh, :, h * D : (h + 1) * D] = dqv[h * TB : (h + 1) * TB, :]
+            out_ref[b, :, (HEADS + h) * D : (HEADS + h + 1) * D] = dqv[h * TB : (h + 1) * TB, :]
         return carry
 
     lax.fori_loop(0, 4, block, 0)
@@ -197,8 +196,12 @@
             yy = lax.rem(y_me - sh + 4, 4)
             i = 2 + nh1 + z * 4 + yy
             half = pl.ds(pl.multiple_of(c * 128, 128), 128)
-            dkv_ref[rel, sh, :, 0:D] = (dkt[i, :, half] * SCALE).T.astype(BF)
-            dkv_ref[rel, sh, :, D:] = dvt[i, :, half].T.astype(BF)
+            if last:
+                ref, at = (keep_ref, send_ref)[rel % 2], rel // 2
+            else:
+                ref, at = (keep_ref, send_ref)[rel // 2], rel % 2
+            ref[at, sh, :, 0:D] = (dkt[i, :, half] * SCALE).T.astype(BF)
+            ref[at, sh, :, D:] = dvt[i, :, half].T.astype(BF)
     for i in range(4):
 
         @pl.when(i < 2 + nh1)
@@ -222,21 +225,18 @@
             hg_ref[f, 64:128, :] = second
 
 
-def span_call(ordinal, pos, cnt, ids, qgs, kvs, hist, acc=None):
-    last = acc is not None
+def span_call(ordinal, pos, cnt, ids, qg, kvs, hist, acc=None):
+    last = ordinal == 1
     smem = pl.BlockSpec(memory_space=pltpu.SMEM)
     vmem = pl.BlockSpec(memory_space=pltpu.VMEM)
     extra = (acc,) if last else ()
     hg = jax.ShapeDtypeStruct((8, 2 * D, TB), BF) if last else jax.ShapeDtypeStruct((8, TB, 2 * D), F32)
     return pl.pallas_call(
-        functools.partial(span_kernel, ordinal, last),
-        out_shape=(
-            jax.ShapeDtypeStruct((4, TB, HEADS * D), BF),
-            jax.ShapeDtypeStruct((4, TB, HEADS * D), BF),
-            jax.ShapeDtypeStruct((4, 4, TB, 2 * D), BF),
-            hg,
-        ),
-        in_specs=[smem] * 3 + [vmem] * (9 + len(extra)),
+        functools.partial(span_kernel, ordinal),
+        out_shape=(jax.ShapeDtypeStruct((4, TB, 2 * HEADS * D), BF),)
+        + (jax.ShapeDtypeStruct((2, 4, TB, 2 * D), BF),) * 2
+        + (hg,),
+        in_specs=[smem] * 3 + [vmem] * (7 + len(extra)),
         out_specs=(vmem,) * 4,
         scratch_shapes=[
             pltpu.VMEM((NROW, 2 * D), BF),
@@ -256,10 +256,60 @@
             pltpu.VMEM((2 * D, NROW), BF),
         ],
         compiler_params=pltpu.CompilerParams(vmem_limit_bytes=56 * 2**20),
-        cost_estimate=pl.CostEstimate(
-            flops=int(2.5e10), bytes_accessed=6 * 2**20, transcendentals=0
-        ),
-    )(pos, cnt, ids, *qgs, *kvs, hist, *extra)
+        cost_estimate=pl.CostEstimate(flops=int(2.5e10), bytes_accessed=6 * 2**20, transcendentals=0),
+    )(pos, cnt, ids, qg, *kvs, *hist, *extra)
+
+
+def split_shifts_kernel(pos_ref, a_ref, b_ref, *outs):
+    for sh in range(4):
+        at = pl.ds(pl.multiple_of(lax.rem(pos_ref[1] + sh, 4) * D, D), D)
+        for j in range(2):
+            outs[sh][j, :, 0:D] = a_ref[0, j, :, at]
+            outs[sh][j, :, D:] = b_ref[0, j, :, at]
+
+
+def join_shifts_kernel(pos_ref, p0, p1, p2, p3, a_ref, b_ref):
+    for sh, part in enumerate((p0, p1, p2, p3)):
+        at = pl.ds(pl.multiple_of(lax.rem(pos_ref[1] + sh, 4) * D, D), D)
+        for j in range(2):
+            a_ref[0, j, :, at] = part[j, :, 0:D]
+            b_ref[0, j, :, at] = part[j, :, D:]
+
+
+def split_heads_kernel(a_ref, b_ref, out0, out1):
+    width = HEADS * D
+    for j, out in enumerate((out0, out1)):
+        for y in range(4):
+            out[y, :, 0:width] = a_ref[0, j, :, y * width : (y + 1) * width]
+            out[y, :, width:] = b_ref[0, j, :, y * width : (y + 1) * width]
+
+
+def join_heads_kernel(in0, in1, a_ref, b_ref):
+    width = HEADS * D
+    for j, part in enumerate((in0, in1)):
+        for y in range(4):
+            a_ref[0, j, :, y * width : (y + 1) * width] = part[y, :, 0:width]
+            b_ref[0, j, :, y * width : (y + 1) * width] = part[y, :, width:]
+
+
+def relayout(kernel, outs, args, with_pos):
+    vmem = pl.BlockSpec(memory_space=pltpu.VMEM)
+    specs = [vmem] * len(args)
+    if with_pos:
+        specs[0] = pl.BlockSpec(memory_space=pltpu.SMEM)
+    size = 2 * sum(a.size * 2 for a in args)
+    return pl.pallas_call(
+        kernel,
+        out_shape=tuple(jax.ShapeDtypeStruct(o, BF) for o in outs),
+        in_specs=specs,
+        out_specs=(vmem,) * len(outs),
+        cost_estimate=pl.CostEstimate(flops=0, bytes_accessed=size, transcendentals=0),
+        compiler_params=pltpu.CompilerParams(vmem_limit_bytes=16 * 2**20),
+    )(*args)
+
+
+def y_exchange(a):
+    return lax.all_to_all(a, "y", split_axis=0, concat_axis=0, tiled=True)
 
 
 def y_shift(a, sh):
@@ -276,68 +326,46 @@
 
 def per_device(queries, span_keys, span_values, cotangent, cache_keys, cache_values, hist_count, span_ids):
     zhi, y_me, core = lax.axis_index("zhi"), lax.axis_index("y"), lax.axis_index("core")
-    f_me = lax.axis_index("x") * 2 + lax.axis_index("zlo")
-    pos = jnp.stack([zhi, y_me, core, f_me]).astype(jnp.int32)
-
-    def head_cols(a, sh, width):
-        target = lax.rem(y_me + sh, 4)
-        return lax.dynamic_slice_in_dim(a, target * width, width, axis=a.ndim - 1)
-
-    kv_sent = [
-        jnp.concatenate([head_cols(span_keys[0], sh, D), head_cols(span_values[0], sh, D)], axis=-1)
-        for sh in range(4)
-    ]
+    pos = jnp.stack([zhi, y_me, core, lax.axis_index("x"), lax.axis_index("zlo")]).astype(jnp.int32)
+
+    cache = jnp.stack([cache_keys.T, cache_values.T])
+    perm = []
+    for head in range(KVH):
+        for p in range(4):
+            perm.append((linear(head // 2, 2 * (head % 2) + p // 2, p % 2), linear(p // 2, head, p % 2)))
+    cache = lax.ppermute(cache, SP, perm)
+    cache = jnp.stack([cache, flip(cache, "zlo")])
+    kv_sent = relayout(split_shifts_kernel, [(2, TB, 2 * D)] * 4, (pos, span_keys, span_values), True)
     kv_own = jnp.stack([kv_sent[0]] + [y_shift(kv_sent[sh], sh) for sh in (1, 2, 3)])
-    cache = jnp.stack([cache_keys.T, cache_values.T])
-    parts = []
-    for k in range(4):
-        perm = []
-        for head in range(KVH):
-            for piece in range(4):
-                src = linear(head // 2, 2 * (head % 2) + piece // 2, piece % 2)
-                to = (piece + k) % 4
-                perm.append((src, linear(to // 2, head, to % 2)))
-        parts.append(lax.ppermute(cache, SP, perm))
-    hist = lax.all_gather(jnp.stack(parts), FS, axis=0, tiled=False).reshape(8, 4, 2, 32, TB)
-
-    def qg_of(j):
-        sent = [
-            jnp.concatenate(
-                [head_cols(queries[0, j], sh, HEADS * D), head_cols(cotangent[0, j], sh, HEADS * D)], axis=-1
-            )
-            for sh in range(4)
-        ]
-        return [sent[0]] + [y_shift(sent[sh], sh) for sh in (1, 2, 3)]
-
-    qg = [qg_of(0), qg_of(1)]
+    kv_own, cache = lax.optimization_barrier((kv_own, cache))
+    kv_z = flip(kv_own, "zhi")
     kv_core = flip(kv_own, "core")
-    kv_z = flip(kv_own, "zhi")
     kv_zc = flip(kv_z, "core")
     kvs = (kv_own, kv_core, kv_z, kv_zc)
-    att0, dq0, dkv0, acc = span_call(0, pos, hist_count, span_ids, qg[0], kvs, hist)
-    att1, dq1, dkv1, hg = span_call(1, pos, hist_count, span_ids, qg[1], kvs, hist, acc)
-
-    def home(a):
-        got = [a[0]] + [y_shift(a[sh], 4 - sh) for sh in (1, 2, 3)]
-        return place(got)
-
-    def place(got):
-        width = got[0].shape[-1]
-        out = jnp.zeros(got[0].shape[:-1] + (4 * width,), got[0].dtype)
-        for sh in range(4):
-            out = lax.dynamic_update_slice_in_dim(out, got[sh], lax.rem(y_me + sh, 4) * width, axis=out.ndim - 1)
-        return out
-
-    def reduce_kv(dkv):
-        total = dkv[0].astype(F32)
-        total += flip(dkv[1], "core").astype(F32)
-        total += flip(dkv[2], "zhi").astype(F32)
-        both = [(linear(z, y, c), linear(1 - z, y, 1 - c)) for z in range(2) for y in range(4) for c in range(2)]
-        total += lax.ppermute(dkv[3], SP, both).astype(F32)
-        return total.astype(BF)
-
-    red = jnp.stack([reduce_kv(dkv0), reduce_kv(dkv1)], axis=1)
+    cache = jnp.stack([cache] + [lax.ppermute(cache, "x", [(i, (i + s) % 4) for i in range(4)]) for s in (1, 2, 3)])
+    cache = jnp.stack([cache, flip(cache, "core")])
+    hist = (cache, flip(cache, "zhi"))
+
+    sent = relayout(split_heads_kernel, [(4, TB, 2 * HEADS * D)] * 2, (queries, cotangent), False)
+    qg = [y_exchange(a) for a in sent]
+    out0, keep0, send0, acc = span_call(0, pos, hist_count, span_ids, qg[0], kvs, hist)
+    out1, keep1, send1, hg = span_call(1, pos, hist_count, span_ids, qg[1], kvs, hist, acc)
+
+    back0 = y_exchange(out0)
+    got0 = flip(send0, "zhi")
+    (out1, send1, hg, back0, got0) = lax.optimization_barrier((out1, send1, hg, back0, got0))
     hg_all = lax.all_to_all(hg, FS, split_axis=0, concat_axis=0, tiled=True)
+    sum0 = (keep0.astype(F32) + got0.astype(F32)).astype(BF)
+    got1 = flip(send1, "core")
+    got0 = flip(sum0[1], "core")
+    sum1 = (keep1.astype(F32) + got1.astype(F32)).astype(BF)
+    got1 = flip(sum1[1], "zhi")
+    back1 = y_exchange(out1)
+    red0 = sum0[0].astype(F32) + got0.astype(F32)
+    red1 = sum1[0].astype(F32) + got1.astype(F32)
+    red = jnp.stack([red0, red1], axis=1).astype(BF)
+    kv_back = [red[0]] + [y_shift(red[sh], 4 - sh) for sh in (1, 2, 3)]
+
     hsum = jnp.sum(hg_all.astype(F32), axis=0).reshape(2, 4, 32, TB)
     mine = []
     for k in range(4):
@@ -350,11 +378,8 @@
         piece = lax.rem(zhi * 2 + core + k, 4)
         mine.append(lax.ppermute(lax.dynamic_index_in_dim(hsum, piece, 1, keepdims=False), SP, perm))
     hgrad = mine[0] + mine[1] + mine[2] + mine[3]
-    attended = jnp.stack([home(att0), home(att1)])[None]
-    grad_q = jnp.stack([home(dq0), home(dq1)])[None]
-    back = [red[0]] + [y_shift(red[sh], 4 - sh) for sh in (1, 2, 3)]
-    grad_k = place([b[..., 0:D] for b in back])[None]
-    grad_v = place([b[..., D:] for b in back])[None]
+    attended, grad_q = relayout(join_heads_kernel, [(1, 2, TB, 4 * HEADS * D)] * 2, (back0, back1), False)
+    grad_k, grad_v = relayout(join_shifts_kernel, [(1, 2, TB, 4 * D)] * 2, (pos, *kv_back), True)
     return attended, grad_q, grad_k, grad_v, hgrad[0].T, hgrad[1].T
 
 

time: 256 us -> 162 us (0.63)
  waiting for transfers between devices: 77.5 us -> 19.2 us
  blocking collectives: 25.2 us -> 0 us
  starting transfers between devices: 96.2 us -> 82.7 us
  Pallas kernels: 37.8 us -> 44.8 us
    ppermute x24 -> x6, waiting for transfers between devices: 55.4 us -> 6.39 us  [y_shift(): return lax.ppermute(a, 'y', [(i, (i + sh) % 4) for i in range(4)])]
    all_gather x1 -> x0, blocking collectives: 25.2 us -> none  [per_device(): lax.all_gather(jnp.stack(parts), FS, axis=0, tiled=False)]
    all_to_all x0 -> x4, starting transfers between devices: none -> 17.8 us  [y_exchange(): return lax.all_to_all(a, 'y', split_axis=0, concat_axis=0, tiled=True)]
    ppermute x6 -> x4, starting transfers between devices: 22.2 us -> 5.46 us  [the longest x3 4.81 us: per_device(): lax.ppermute(cache, 'x', [(i, (i + s) % 4) for i in range(4)])]
    ppermute x24 -> x6, starting transfers between devices: 26.2 us -> 14.2 us  [y_shift(): return lax.ppermute(a, 'y', [(i, (i + sh) % 4) for i in range(4)])]
    ppermute x7 -> x10, starting transfers between devices: 32.8 us -> 23.1 us  [flip(): return lax.ppermute(a, axis, [(0, 1), (1, 0)])]
    ppermute x4, starting transfers between devices: 8.7 us -> 18 us  [per_device(): lax.ppermute(lax.dynamic_index_in_dim(hsum, piece, 1, keepdims=False), SP...]
    ppermute x6 -> x4, waiting for transfers between devices: 8.54 us -> 0.01 us  [the longest x3 0.01 us: per_device(): lax.ppermute(cache, 'x', [(i, (i + s) % 4) for i in range(4)])]
  transfers between devices with their start and end apart: 42 -> 29, of which waited for: 21 -> 10; matrix products, arithmetic and copies ran while one was open for 3% -> 3% of each run, Pallas kernels for 7% -> 27%
where the time goes in v2:
time: 162 us; the launch traced here: 160 us
  starting transfers between devices  82.7 us (51%)
  Pallas kernels  44.8 us (28%)
  waiting for transfers between devices  19.2 us (12%)
  local copies, waits for them, and re-layouts  8.67 us (5%)
  other arithmetic  3.52 us (2%)
    pallas_call x2, Pallas kernels, span_call(): pl.pallas_call(functools.partial(span_kernel, ordinal), out_shape=(jax.Sh...  39.8 us
    ppermute x10, starting transfers between devices, flip(): return lax.ppermute(a, axis, [(0, 1), (1, 0)])  23.1 us
    ppermute x4, starting transfers between devices, per_device(): lax.ppermute(lax.dynamic_index_in_dim(hsum, piece, 1, keepdims=False), SP...  18 us
    all_to_all x4, starting transfers between devices, y_exchange(): return lax.all_to_all(a, 'y', split_axis=0, concat_axis=0, tiled=True)  17.8 us
    ppermute x6, starting transfers between devices, y_shift(): return lax.ppermute(a, 'y', [(i, (i + sh) % 4) for i in range(4)])  14.2 us
    ppermute x10, waiting for transfers between devices, flip(): return lax.ppermute(a, axis, [(0, 1), (1, 0)])  9.16 us
    unnamed x31, local copies, waits for them, and re-layouts  7.21 us
    ppermute x6, waiting for transfers between devices, y_shift(): return lax.ppermute(a, 'y', [(i, (i + sh) % 4) for i in range(4)])  6.39 us
  transfers between devices with their start and end apart: 29, of which 10 were waited for; matrix products, arithmetic and copies ran while one was open for 3% of the time, Pallas kernels for 27%

profile of v2, /device:TPU:1, one launch (start us, length us, event | category | flops | bytes accessed | tf_op | source)
XLA Modules:
  0.0 159.8 jit_solution(6370547104263078905)
XLA Ops:
  0.6 0.8 pad_maximum_fusion.5
  1.4 0.7 collective-permute-start.3
  2.1 0.1 stack.92.pos_ref
  2.2 0.9 copy-done.2
  3.2 0.9 copy-done.3
  4.1 0.6 shard_map.128
  4.8 6.9 %collective-permute-start = (bf16[2,128,256]{2,1,0:T(8,128)(2,1)S(1)}, bf16[2,128,256]{2,1,0:T(8,128)(2,1)S(1)}, u32[]{:S(2)}, u32[]{:S(2)}) collective-permute-start(bf16[2,128,256]{2,1,0:T(8,128)(2,1)S(1)} %get-tuple-element.33), channel_id=1, source_target_pairs={{0,2},{2,4},{4,6},{6,0},{1,3},{3,5},{5,7},{7,1},{8,10},{10,12},{12... | collective-permute-start | bytes 393224 | tf_op jit(solution)/shard_map/ppermute | solution.py:316
  11.7 3.4 %collective-permute-start.1 = (bf16[2,128,256]{2,1,0:T(8,128)(2,1)S(1)}, bf16[2,128,256]{2,1,0:T(8,128)(2,1)S(1)}, u32[]{:S(2)}, u32[]{:S(2)}) collective-permute-start(bf16[2,128,256]{2,1,0:T(8,128)(2,1)S(1)} %get-tuple-element.34), channel_id=1, source_target_pairs={{0,4},{2,6},{4,0},{6,2},{1,5},{3,7},{5,1},{7,3},{8,12},{10,14},{12... | collective-permute-start | bytes 393224 | tf_op jit(solution)/shard_map/ppermute | solution.py:316
  15.1 0.7 collective-permute-start.4
  15.8 2.1 %collective-permute-done.4 = bf16[2,32,128]{2,1,0:T(8,128)(2,1)S(1)} collective-permute-done((bf16[2,32,128]{2,1,0:T(8,128)(2,1)S(1)}, bf16[2,32,128]{2,1,0:T(8,128)(2,1)S(1)}, u32[]{:S(2)}, u32[]{:S(2)}) %collective-permute-start.4) | collective-permute-done | bytes 16416 | tf_op jit(solution)/shard_map/ppermute | solution.py:320
  18.0 0.0 collective-permute-done
  18.0 2.2 %collective-permute-done.1 = bf16[2,128,256]{2,1,0:T(8,128)(2,1)S(1)} collective-permute-done((bf16[2,128,256]{2,1,0:T(8,128)(2,1)S(1)}, bf16[2,128,256]{2,1,0:T(8,128)(2,1)S(1)}, u32[]{:S(2)}, u32[]{:S(2)}) %collective-permute-start.1) | collective-permute-done | bytes 131104 | tf_op jit(solution)/shard_map/ppermute | solution.py:316
  20.2 0.1 collective-permute-done.2
  20.3 0.1 pad_maximum_fusion.kv0
  20.3 0.7 collective-permute-start.6
  21.0 1.2 copy-done.1
  22.3 1.5 shard_map.127
  23.7 4.8 %all-to-all-start.1 = ((bf16[4,128,1024]{2,1,0:T(8,128)(2,1)}), bf16[4,128,1024]{2,1,0:T(8,128)(2,1)S(1)}, u32[]{:S(2)}, u32[]{:S(2)}) async-start(bf16[4,128,1024]{2,1,0:T(8,128)(2,1)} %get-tuple-element.38), calls=%async_computation.1 | async-start | bytes 2097152 | tf_op jit(solution)/shard_map/all_to_all | solution.py:312
  28.6 1.2 collective-permute-start.8
  29.8 2.5 %collective-permute-start.9 = (bf16[2,2,32,128]{3,2,1,0:T(8,128)(2,1)S(1)}, bf16[2,2,32,128]{3,2,1,0:T(8,128)(2,1)S(1)}, u32[]{:S(2)}, u32[]{:S(2)}) collective-permute-start(bf16[2,2,32,128]{3,2,1,0:T(8,128)(2,1)S(1)} %pad_maximum_fusion.4), channel_id=1, source_target_pairs={{0,64},{32,96},{64,0},{96,32},{1,65},{33,97},{65,1},{97,33},{2,66}... | collective-permute-start | bytes 98312 | tf_op jit(solution)/shard_map/ppermute | solution.py:345
  32.2 1.2 collective-permute-start.10
  33.4 2.4 %collective-permute-start.5 = (bf16[4,2,128,256]{3,2,1,0:T(8,128)(2,1)S(1)}, bf16[4,2,128,256]{3,2,1,0:T(8,128)(2,1)}, u32[]{:S(2)}, u32[]{:S(2)}) collective-permute-start(bf16[4,2,128,256]{3,2,1,0:T(8,128)(2,1)S(1)} %pad_maximum_fusion.kv0), channel_id=1, source_target_pairs={{0,1},{1,0},{2,3},{3,2},{4,5},{5,4},{6,7},{7,6},{8,9},{9,8},{10,11... | collective-permute-start | bytes 1572872 | tf_op jit(solution)/shard_map/ppermute | solution.py:320
  35.8 0.0 collective-permute-done.6.kv2
  35.8 0.5 collective-permute-start.7
  36.3 2.0 %collective-permute-start.11 = (bf16[4,2,2,32,128]{4,3,2,1,0:T(8,128)(2,1)S(1)}, bf16[4,2,2,32,128]{4,3,2,1,0:T(8,128)(2,1)S(1)}, u32[]{:S(2)}, u32[]{:S(2)}) collective-permute-start(bf16[4,2,2,32,128]{4,3,2,1,0:T(8,128)(2,1)S(1)} %get-tuple-element.65), channel_id=1, source_target_pairs={{0,1},{1,0},{2,3},{3,2},{4,5},{5,4},{6,7},{7,6},{8,9},{9,8},{10,11... | collective-permute-start | bytes 393224 | tf_op jit(solution)/shard_map/ppermute | solution.py:320
  38.4 1.0 collective-permute-done.11
  39.4 0.0 copy-start.12
  39.4 2.0 %collective-permute-start.12 = (bf16[2,4,2,2,32,128]{5,4,3,2,1,0:T(8,128)(2,1)S(1)}, bf16[2,4,2,2,32,128]{5,4,3,2,1,0:T(8,128)(2,1)}, u32[]{:S(2)}, u32[]{:S(2)}) collective-permute-start(bf16[2,4,2,2,32,128]{5,4,3,2,1,0:T(8,128)(2,1)S(1)} %pad_maximum_fusion.1.h0), channel_id=1, source_target_pairs={{0,8},{8,0},{1,9},{9,1},{2,10},{10,2},{3,11},{11,3},{4,12},{12,4},... | collective-permute-start | bytes 786440 | tf_op jit(solution)/shard_map/ppermute | solution.py:320
  41.4 0.7 copy-done.13
  42.1 0.7 copy.17.ids_ref
  42.8 1.0 copy-done.6
  43.7 4.4 %all-to-all-start = ((bf16[4,128,1024]{2,1,0:T(8,128)(2,1)}), bf16[4,128,1024]{2,1,0:T(8,128)(2,1)S(1)}, u32[]{:S(2)}, u32[]{:S(2)}) async-start(bf16[4,128,1024]{2,1,0:T(8,128)(2,1)} %get-tuple-element.31), calls=%async_computation | async-start | bytes 2097152 | tf_op jit(solution)/shard_map/all_to_all | solution.py:312
  48.2 0.4 collective-permute-done.12.h1
  48.6 19.8 %shard_map.129 = (bf16[4,128,1024]{2,1,0:T(8,128)(2,1)}, bf16[2,4,128,256]{3,2,1,0:T(8,128)(2,1)}, bf16[2,4,128,256]{3,2,1,0:T(8,128)(2,1)}, f32[8,128,256]{2,1,0:T(8,128)}) custom-call(s32[5]{0:T(128)} %copy-done.4, s32[8]{0:T(128)} %cnt_ref.3, s32[8,2]{1,0:T(8,128)} %copy.17.ids_ref, bf16[4,128,1024]{2,1,0:T(8,128)(2,1)} %copy-done.6, ...), custom_call_target="tpu_custom_call" | custom-call | flops 24999999488 | bytes 6291456 | tf_op jit(solution)/shard_map/pallas_call | solution.py:234
  68.4 9.5 %collective-permute-start.13 = (bf16[2,4,128,256]{3,2,1,0:T(8,128)(2,1)}, bf16[2,4,128,256]{3,2,1,0:T(8,128)(2,1)S(1)}, u32[]{:S(2)}, u32[]{:S(2)}) collective-permute-start(bf16[2,4,128,256]{3,2,1,0:T(8,128)(2,1)} %get-tuple-element.44), channel_id=1, source_target_pairs={{0,8},{8,0},{1,9},{9,1},{2,10},{10,2},{3,11},{11,3},{4,12},{12,4},... | collective-permute-start | bytes 1572872 | tf_op jit(solution)/shard_map/ppermute | solution.py:320
  77.9 1.0 copy-done.7
  78.9 4.4 %all-to-all-start.2 = ((bf16[4,128,1024]{2,1,0:T(8,128)(2,1)}), bf16[4,128,1024]{2,1,0:T(8,128)(2,1)S(1)}, u32[]{:S(2)}, u32[]{:S(2)}) async-start(bf16[4,128,1024]{2,1,0:T(8,128)(2,1)} %get-tuple-element.43), calls=%async_computation.2 | async-start | bytes 2097152 | tf_op jit(solution)/shard_map/all_to_all | solution.py:312
  83.3 20.0 %shard_map.130 = (bf16[4,128,1024]{2,1,0:T(8,128)(2,1)}, bf16[2,4,128,256]{3,2,1,0:T(8,128)(2,1)}, bf16[2,4,128,256]{3,2,1,0:T(8,128)(2,1)}, bf16[8,256,128]{2,1,0:T(8,128)(2,1)}) custom-call(s32[5]{0:T(128)} %copy-done.4, s32[8]{0:T(128)} %cnt_ref.3, s32[8,2]{1,0:T(8,128)} %copy.17.ids_ref, bf16[4,128,1024]{2,1,0:T(8,128)(2,1)} %copy-done.7, ...), custom_call_target="tpu_custom_call" | custom-call | flops 24999999488 | bytes 6291456 | tf_op jit(solution)/shard_map/pallas_call | solution.py:234
  103.3 0.8 copy-done.10
  104.1 4.1 %all-to-all-start.4 = ((bf16[8,256,128]{2,1,0:T(8,128)(2,1)}), bf16[8,256,128]{2,1,0:T(8,128)(2,1)S(1)}, u32[]{:S(2)}, u32[]{:S(2)}) async-start(bf16[8,256,128]{2,1,0:T(8,128)(2,1)} %get-tuple-element.55), calls=%async_computation.4 | async-start | bytes 1048576 | tf_op jit(solution)/shard_map/all_to_all | solution.py:357
  108.2 2.0 %collective-permute-start.15 = (bf16[2,4,128,256]{3,2,1,0:T(8,128)(2,1)}, bf16[2,4,128,256]{3,2,1,0:T(8,128)(2,1)}, u32[]{:S(2)}, u32[]{:S(2)}) collective-permute-start(bf16[2,4,128,256]{3,2,1,0:T(8,128)(2,1)} %get-tuple-element.52), channel_id=1, source_target_pairs={{0,1},{1,0},{2,3},{3,2},{4,5},{5,4},{6,7},{7,6},{8,9},{9,8},{10,11... | collective-permute-start | bytes 1572872 | tf_op jit(solution)/shard_map/ppermute | solution.py:320
  110.2 1.2 add_convert_fusion.1
  111.4 0.7 slice_bitcast_fusion.2
  112.1 0.0 collective-permute-start.14
  112.1 3.2 %all-to-all-done.4 = bf16[8,256,128]{2,1,0:T(8,128)(2,1)S(1)} async-done(((bf16[8,256,128]{2,1,0:T(8,128)(2,1)}), bf16[8,256,128]{2,1,0:T(8,128)(2,1)S(1)}, u32[]{:S(2)}, u32[]{:S(2)}) %all-to-all-start.4) | async-done | bytes 524320 | tf_op jit(solution)/shard_map/all_to_all | solution.py:357
  115.3 4.2 %all-to-all-start.3 = ((bf16[4,128,1024]{2,1,0:T(8,128)(2,1)}), bf16[4,128,1024]{2,1,0:T(8,128)(2,1)S(1)}, u32[]{:S(2)}, u32[]{:S(2)}) async-start(bf16[4,128,1024]{2,1,0:T(8,128)(2,1)} %get-tuple-element.46), calls=%async_computation.3 | async-start | bytes 2097152 | tf_op jit(solution)/shard_map/all_to_all | solution.py:312
  119.5 0.1 convert_reduce_fusion
  119.6 0.8 collective-permute-start.20
  120.4 8.2 %collective-permute-start.21 = (f32[2,32,128]{2,1,0:T(8,128)S(1)}, f32[2,32,128]{2,1,0:T(8,128)S(1)}, u32[]{:S(2)}, u32[]{:S(2)}) collective-permute-start(f32[2,32,128]{2,1,0:T(8,128)S(1)} %get-tuple-element.60), channel_id=1, source_target_pairs={{0,1},{1,2},{8,3},{9,0},{2,5},{3,6},{10,7},{11,4},{4,9},{5,10},{12... | collective-permute-start | bytes 98312 | tf_op jit(solution)/shard_map/ppermute | solution.py:379
  128.6 9.0 %collective-permute-start.22 = (f32[2,32,128]{2,1,0:T(8,128)S(1)}, f32[2,32,128]{2,1,0:T(8,128)S(1)}, u32[]{:S(2)}, u32[]{:S(2)}) collective-permute-start(f32[2,32,128]{2,1,0:T(8,128)S(1)} %get-tuple-element.62), channel_id=1, source_target_pairs={{0,2},{1,3},{8,0},{9,1},{2,6},{3,7},{10,4},{11,5},{4,10},{5,11},{1... | collective-permute-start | bytes 98312 | tf_op jit(solution)/shard_map/ppermute | solution.py:379
  137.7 1.2 add_convert_fusion
  138.9 3.1 %collective-permute-start.16 = (bf16[4,128,256]{2,1,0:T(8,128)(2,1)S(1)}, bf16[4,128,256]{2,1,0:T(8,128)(2,1)S(1)}, u32[]{:S(2)}, u32[]{:S(2)}) collective-permute-start(bf16[4,128,256]{2,1,0:T(8,128)(2,1)S(1)} %slice_bitcast_fusion), channel_id=1, source_target_pairs={{0,8},{8,0},{1,9},{9,1},{2,10},{10,2},{3,11},{11,3},{4,12},{12,4},... | collective-permute-start | bytes 786440 | tf_op jit(solution)/shard_map/ppermute | solution.py:320
  142.0 0.1 fusion.2
  142.1 0.4 collective-permute-done.23
  142.5 5.6 %collective-permute-done.16 = bf16[4,128,256]{2,1,0:T(8,128)(2,1)S(1)} collective-permute-done((bf16[4,128,256]{2,1,0:T(8,128)(2,1)S(1)}, bf16[4,128,256]{2,1,0:T(8,128)(2,1)S(1)}, u32[]{:S(2)}, u32[]{:S(2)}) %collective-permute-start.16) | collective-permute-done | bytes 262176 | tf_op jit(solution)/shard_map/ppermute | solution.py:320
  148.1 0.1 fusion.3
  148.2 1.0 collective-permute-start.17
  149.2 2.1 %collective-permute-start.18 = (bf16[2,128,256]{2,1,0:T(8,128)(2,1)S(1)}, bf16[2,128,256]{2,1,0:T(8,128)(2,1)S(1)}, u32[]{:S(2)}, u32[]{:S(2)}) collective-permute-start(bf16[2,128,256]{2,1,0:T(8,128)(2,1)S(1)} %get-tuple-element.59), channel_id=1, source_target_pairs={{0,4},{2,6},{4,0},{6,2},{1,5},{3,7},{5,1},{7,3},{8,12},{10,14},{12... | collective-permute-start | bytes 393224 | tf_op jit(solution)/shard_map/ppermute | solution.py:316
  151.3 0.8 collective-permute-start.19
  152.1 0.6 slice_bitcast_fusion.4
  152.7 1.5 shard_map.131
  154.2 0.3 collective-permute-done.18.p2
  154.5 3.8 %collective-permute-done.19.p3 = bf16[2,128,256]{2,1,0:T(8,128)(2,1)S(1)} collective-permute-done((bf16[2,128,256]{2,1,0:T(8,128)(2,1)S(1)}, bf16[2,128,256]{2,1,0:T(8,128)(2,1)S(1)}, u32[]{:S(2)}, u32[]{:S(2)}) %collective-permute-start.19) | collective-permute-done | bytes 131104 | tf_op jit(solution)/shard_map/ppermute | solution.py:316
  158.3 1.4 shard_map.132
  (48 shorter events, 0.2 us)
Async XLA Ops:
  0.6 20.4 %copy-start = (bf16[1,2,128,2048]{3,2,1,0:T(8,128)(2,1)S(1)}, bf16[1,2,128,2048]{3,2,1,0:T(8,128)(2,1)}, u32[]{:S(2)}) copy-start(bf16[1,2,128,2048]{3,2,1,0:T(8,128)(2,1)} %a_ref.2) | copy-start | bytes 3145732
  1.4 13.7 %collective-permute-start.3 = (bf16[2,32,128]{2,1,0:T(8,128)(2,1)S(1)}, bf16[2,32,128]{2,1,0:T(8,128)(2,1)S(1)}, u32[]{:S(2)}, u32[]{:S(2)}) collective-permute-start(bf16[2,32,128]{2,1,0:T(8,128)(2,1)S(1)} %pad_maximum_fusion.5), channel_id=1, source_target_pairs={{0,0},{1,1},{2,8},{3,9},{4,2},{5,3},{6,10},{7,11},{8,4},{9,5},{10,... | collective-permute-start | bytes 49160 | tf_op jit(solution)/shard_map/ppermute | solution.py:336
  2.2 1.0 copy-start.2
  3.2 0.9 copy-start.3
  4.1 0.7 copy-start.4
  4.8 13.2 %collective-permute-start = (bf16[2,128,256]{2,1,0:T(8,128)(2,1)S(1)}, bf16[2,128,256]{2,1,0:T(8,128)(2,1)S(1)}, u32[]{:S(2)}, u32[]{:S(2)}) collective-permute-start(bf16[2,128,256]{2,1,0:T(8,128)(2,1)S(1)} %get-tuple-element.33), channel_id=1, source_target_pairs={{0,2},{2,4},{4,6},{6,0},{1,3},{3,5},{5,7},{7,1},{8,10},{10,12},{12... | collective-permute-start | bytes 393224 | tf_op jit(solution)/shard_map/ppermute | solution.py:316
  11.7 8.5 %collective-permute-start.1 = (bf16[2,128,256]{2,1,0:T(8,128)(2,1)S(1)}, bf16[2,128,256]{2,1,0:T(8,128)(2,1)S(1)}, u32[]{:S(2)}, u32[]{:S(2)}) collective-permute-start(bf16[2,128,256]{2,1,0:T(8,128)(2,1)S(1)} %get-tuple-element.34), channel_id=1, source_target_pairs={{0,4},{2,6},{4,0},{6,2},{1,5},{3,7},{5,1},{7,3},{8,12},{10,14},{12... | collective-permute-start | bytes 393224 | tf_op jit(solution)/shard_map/ppermute | solution.py:316
  15.1 5.2 %collective-permute-start.2 = (bf16[2,128,256]{2,1,0:T(8,128)(2,1)S(1)}, bf16[2,128,256]{2,1,0:T(8,128)(2,1)S(1)}, u32[]{:S(2)}, u32[]{:S(2)}) collective-permute-start(bf16[2,128,256]{2,1,0:T(8,128)(2,1)S(1)} %get-tuple-element.35), channel_id=1, source_target_pairs={{0,6},{2,0},{4,2},{6,4},{1,7},{3,1},{5,3},{7,5},{8,14},{10,8},{12,... | collective-permute-start | bytes 393224 | tf_op jit(solution)/shard_map/ppermute | solution.py:316
  15.1 2.9 %collective-permute-start.4 = (bf16[2,32,128]{2,1,0:T(8,128)(2,1)S(1)}, bf16[2,32,128]{2,1,0:T(8,128)(2,1)S(1)}, u32[]{:S(2)}, u32[]{:S(2)}) collective-permute-start(bf16[2,32,128]{2,1,0:T(8,128)(2,1)S(1)} %collective-permute-done.3), channel_id=1, source_target_pairs={{0,16},{16,0},{1,17},{17,1},{2,18},{18,2},{3,19},{19,3},{4,20},{20... | collective-permute-start | bytes 49160 | tf_op jit(solution)/shard_map/ppermute | solution.py:320
  20.3 13.1 %copy-start.11 = (bf16[4,2,128,256]{3,2,1,0:T(8,128)(2,1)}, bf16[4,2,128,256]{3,2,1,0:T(8,128)(2,1)S(1)}, u32[]{:S(2)}) copy-start(bf16[4,2,128,256]{3,2,1,0:T(8,128)(2,1)S(1)} %pad_maximum_fusion.kv0) | copy-start | bytes 1572868
  20.3 15.4 %collective-permute-start.6 = (bf16[4,2,128,256]{3,2,1,0:T(8,128)(2,1)S(1)}, bf16[4,2,128,256]{3,2,1,0:T(8,128)(2,1)S(1)}, u32[]{:S(2)}, u32[]{:S(2)}) collective-permute-start(bf16[4,2,128,256]{3,2,1,0:T(8,128)(2,1)S(1)} %pad_maximum_fusion.kv0), channel_id=1, source_target_pairs={{0,8},{8,0},{1,9},{9,1},{2,10},{10,2},{3,11},{11,3},{4,12},{12,4},... | collective-permute-start | bytes 1572872 | tf_op jit(solution)/shard_map/ppermute | solution.py:320
  21.0 1.2 copy-start.1
  23.7 19.0 %all-to-all-start.1 = ((bf16[4,128,1024]{2,1,0:T(8,128)(2,1)}), bf16[4,128,1024]{2,1,0:T(8,128)(2,1)S(1)}, u32[]{:S(2)}, u32[]{:S(2)}) async-start(bf16[4,128,1024]{2,1,0:T(8,128)(2,1)} %get-tuple-element.38), calls=%async_computation.1 | async-start | bytes 2097152 | tf_op jit(solution)/shard_map/all_to_all | solution.py:312
  28.6 7.7 %collective-permute-start.8 = (bf16[2,2,32,128]{3,2,1,0:T(8,128)(2,1)S(1)}, bf16[2,2,32,128]{3,2,1,0:T(8,128)(2,1)S(1)}, u32[]{:S(2)}, u32[]{:S(2)}) collective-permute-start(bf16[2,2,32,128]{3,2,1,0:T(8,128)(2,1)S(1)} %pad_maximum_fusion.4), channel_id=1, source_target_pairs={{0,32},{32,64},{64,96},{96,0},{1,33},{33,65},{65,97},{97,1},{2,34}... | collective-permute-start | bytes 98312 | tf_op jit(solution)/shard_map/ppermute | solution.py:345
  29.8 6.5 %collective-permute-start.9 = (bf16[2,2,32,128]{3,2,1,0:T(8,128)(2,1)S(1)}, bf16[2,2,32,128]{3,2,1,0:T(8,128)(2,1)S(1)}, u32[]{:S(2)}, u32[]{:S(2)}) collective-permute-start(bf16[2,2,32,128]{3,2,1,0:T(8,128)(2,1)S(1)} %pad_maximum_fusion.4), channel_id=1, source_target_pairs={{0,64},{32,96},{64,0},{96,32},{1,65},{33,97},{65,1},{97,33},{2,66}... | collective-permute-start | bytes 98312 | tf_op jit(solution)/shard_map/ppermute | solution.py:345
  32.2 4.0 %collective-permute-start.10 = (bf16[2,2,32,128]{3,2,1,0:T(8,128)(2,1)S(1)}, bf16[2,2,32,128]{3,2,1,0:T(8,128)(2,1)S(1)}, u32[]{:S(2)}, u32[]{:S(2)}) collective-permute-start(bf16[2,2,32,128]{3,2,1,0:T(8,128)(2,1)S(1)} %pad_maximum_fusion.4), channel_id=1, source_target_pairs={{0,96},{32,0},{64,32},{96,64},{1,97},{33,1},{65,33},{97,65},{2,98}... | collective-permute-start | bytes 98312 | tf_op jit(solution)/shard_map/ppermute | solution.py:345
  33.4 15.2 %collective-permute-start.5 = (bf16[4,2,128,256]{3,2,1,0:T(8,128)(2,1)S(1)}, bf16[4,2,128,256]{3,2,1,0:T(8,128)(2,1)}, u32[]{:S(2)}, u32[]{:S(2)}) collective-permute-start(bf16[4,2,128,256]{3,2,1,0:T(8,128)(2,1)S(1)} %pad_maximum_fusion.kv0), channel_id=1, source_target_pairs={{0,1},{1,0},{2,3},{3,2},{4,5},{5,4},{6,7},{7,6},{8,9},{9,8},{10,11... | collective-permute-start | bytes 1572872 | tf_op jit(solution)/shard_map/ppermute | solution.py:320
  35.8 7.0 %copy-start.14 = (bf16[4,2,128,256]{3,2,1,0:T(8,128)(2,1)}, bf16[4,2,128,256]{3,2,1,0:T(8,128)(2,1)S(1)}, u32[]{:S(2)}) copy-start(bf16[4,2,128,256]{3,2,1,0:T(8,128)(2,1)S(1)} %collective-permute-done.6.kv2) | copy-start | bytes 1572868
  35.8 12.8 %collective-permute-start.7 = (bf16[4,2,128,256]{3,2,1,0:T(8,128)(2,1)S(1)}, bf16[4,2,128,256]{3,2,1,0:T(8,128)(2,1)}, u32[]{:S(2)}, u32[]{:S(2)}) collective-permute-start(bf16[4,2,128,256]{3,2,1,0:T(8,128)(2,1)S(1)} %collective-permute-done.6.kv2), channel_id=1, source_target_pairs={{0,1},{1,0},{2,3},{3,2},{4,5},{5,4},{6,7},{7,6},{8,9},{9,8},{10,11... | collective-permute-start | bytes 1572872 | tf_op jit(solution)/shard_map/ppermute | solution.py:320
  36.3 3.0 %collective-permute-start.11 = (bf16[4,2,2,32,128]{4,3,2,1,0:T(8,128)(2,1)S(1)}, bf16[4,2,2,32,128]{4,3,2,1,0:T(8,128)(2,1)S(1)}, u32[]{:S(2)}, u32[]{:S(2)}) collective-permute-start(bf16[4,2,2,32,128]{4,3,2,1,0:T(8,128)(2,1)S(1)} %get-tuple-element.65), channel_id=1, source_target_pairs={{0,1},{1,0},{2,3},{3,2},{4,5},{5,4},{6,7},{7,6},{8,9},{9,8},{10,11... | collective-permute-start | bytes 393224 | tf_op jit(solution)/shard_map/ppermute | solution.py:320
  39.4 3.4 %copy-start.12 = (bf16[2,4,2,2,32,128]{5,4,3,2,1,0:T(8,128)(2,1)}, bf16[2,4,2,2,32,128]{5,4,3,2,1,0:T(8,128)(2,1)S(1)}, u32[]{:S(2)}) copy-start(bf16[2,4,2,2,32,128]{5,4,3,2,1,0:T(8,128)(2,1)S(1)} %pad_maximum_fusion.1.h0) | copy-start | bytes 786436
  39.4 9.2 %collective-permute-start.12 = (bf16[2,4,2,2,32,128]{5,4,3,2,1,0:T(8,128)(2,1)S(1)}, bf16[2,4,2,2,32,128]{5,4,3,2,1,0:T(8,128)(2,1)}, u32[]{:S(2)}, u32[]{:S(2)}) collective-permute-start(bf16[2,4,2,2,32,128]{5,4,3,2,1,0:T(8,128)(2,1)S(1)} %pad_maximum_fusion.1.h0), channel_id=1, source_target_pairs={{0,8},{8,0},{1,9},{9,1},{2,10},{10,2},{3,11},{11,3},{4,12},{12,4},... | collective-permute-start | bytes 786440 | tf_op jit(solution)/shard_map/ppermute | solution.py:320
  41.4 0.7 copy-start.13
  42.8 1.0 copy-start.6
  43.7 34.2 %all-to-all-start = ((bf16[4,128,1024]{2,1,0:T(8,128)(2,1)}), bf16[4,128,1024]{2,1,0:T(8,128)(2,1)S(1)}, u32[]{:S(2)}, u32[]{:S(2)}) async-start(bf16[4,128,1024]{2,1,0:T(8,128)(2,1)} %get-tuple-element.31), calls=%async_computation | async-start | bytes 2097152 | tf_op jit(solution)/shard_map/all_to_all | solution.py:312
  68.4 34.9 %collective-permute-start.13 = (bf16[2,4,128,256]{3,2,1,0:T(8,128)(2,1)}, bf16[2,4,128,256]{3,2,1,0:T(8,128)(2,1)S(1)}, u32[]{:S(2)}, u32[]{:S(2)}) collective-permute-start(bf16[2,4,128,256]{3,2,1,0:T(8,128)(2,1)} %get-tuple-element.44), channel_id=1, source_target_pairs={{0,8},{8,0},{1,9},{9,1},{2,10},{10,2},{3,11},{11,3},{4,12},{12,4},... | collective-permute-start | bytes 1572872 | tf_op jit(solution)/shard_map/ppermute | solution.py:320
  77.9 1.0 copy-start.7
  78.9 24.4 %all-to-all-start.2 = ((bf16[4,128,1024]{2,1,0:T(8,128)(2,1)}), bf16[4,128,1024]{2,1,0:T(8,128)(2,1)S(1)}, u32[]{:S(2)}, u32[]{:S(2)}) async-start(bf16[4,128,1024]{2,1,0:T(8,128)(2,1)} %get-tuple-element.43), calls=%async_computation.2 | async-start | bytes 2097152 | tf_op jit(solution)/shard_map/all_to_all | solution.py:312
  103.3 0.8 copy-start.10
  103.3 6.9 %copy-start.9 = (bf16[2,4,128,256]{3,2,1,0:T(8,128)(2,1)S(1)}, bf16[2,4,128,256]{3,2,1,0:T(8,128)(2,1)}, u32[]{:S(2)}) copy-start(bf16[2,4,128,256]{3,2,1,0:T(8,128)(2,1)} %get-tuple-element.49) | copy-start | bytes 1572868
  104.1 11.3 %all-to-all-start.4 = ((bf16[8,256,128]{2,1,0:T(8,128)(2,1)}), bf16[8,256,128]{2,1,0:T(8,128)(2,1)S(1)}, u32[]{:S(2)}, u32[]{:S(2)}) async-start(bf16[8,256,128]{2,1,0:T(8,128)(2,1)} %get-tuple-element.55), calls=%async_computation.4 | async-start | bytes 1048576 | tf_op jit(solution)/shard_map/all_to_all | solution.py:357
  108.2 29.5 %collective-permute-start.15 = (bf16[2,4,128,256]{3,2,1,0:T(8,128)(2,1)}, bf16[2,4,128,256]{3,2,1,0:T(8,128)(2,1)}, u32[]{:S(2)}, u32[]{:S(2)}) collective-permute-start(bf16[2,4,128,256]{3,2,1,0:T(8,128)(2,1)} %get-tuple-element.52), channel_id=1, source_target_pairs={{0,1},{1,0},{2,3},{3,2},{4,5},{5,4},{6,7},{7,6},{8,9},{9,8},{10,11... | collective-permute-start | bytes 1572872 | tf_op jit(solution)/shard_map/ppermute | solution.py:320
  112.1 26.8 %collective-permute-start.14 = (bf16[4,128,256]{2,1,0:T(8,128)(2,1)}, bf16[4,128,256]{2,1,0:T(8,128)(2,1)S(1)}, u32[]{:S(2)}, u32[]{:S(2)}) collective-permute-start(bf16[4,128,256]{2,1,0:T(8,128)(2,1)} %slice_bitcast_fusion.2), channel_id=1, source_target_pairs={{0,1},{1,0},{2,3},{3,2},{4,5},{5,4},{6,7},{7,6},{8,9},{9,8},{10,11... | collective-permute-start | bytes 786440 | tf_op jit(solution)/shard_map/ppermute | solution.py:320
  115.3 37.4 %all-to-all-start.3 = ((bf16[4,128,1024]{2,1,0:T(8,128)(2,1)}), bf16[4,128,1024]{2,1,0:T(8,128)(2,1)S(1)}, u32[]{:S(2)}, u32[]{:S(2)}) async-start(bf16[4,128,1024]{2,1,0:T(8,128)(2,1)} %get-tuple-element.46), calls=%async_computation.3 | async-start | bytes 2097152 | tf_op jit(solution)/shard_map/all_to_all | solution.py:312
  119.5 18.1 %copy-start.8 = (bf16[2,4,128,256]{3,2,1,0:T(8,128)(2,1)S(1)}, bf16[2,4,128,256]{3,2,1,0:T(8,128)(2,1)}, u32[]{:S(2)}) copy-start(bf16[2,4,128,256]{3,2,1,0:T(8,128)(2,1)} %get-tuple-element.51) | copy-start | bytes 1572868
  119.6 22.4 %collective-permute-start.20 = (f32[2,32,128]{2,1,0:T(8,128)S(1)}, f32[2,32,128]{2,1,0:T(8,128)S(1)}, u32[]{:S(2)}, u32[]{:S(2)}) collective-permute-start(f32[2,32,128]{2,1,0:T(8,128)S(1)} %get-tuple-element.63), channel_id=1, source_target_pairs={{0,0},{1,1},{8,2},{9,3},{2,4},{3,5},{10,6},{11,7},{4,8},{5,9},{12,... | collective-permute-start | bytes 98312 | tf_op jit(solution)/shard_map/ppermute | solution.py:379
  120.4 21.6 %collective-permute-start.21 = (f32[2,32,128]{2,1,0:T(8,128)S(1)}, f32[2,32,128]{2,1,0:T(8,128)S(1)}, u32[]{:S(2)}, u32[]{:S(2)}) collective-permute-start(f32[2,32,128]{2,1,0:T(8,128)S(1)} %get-tuple-element.60), channel_id=1, source_target_pairs={{0,1},{1,2},{8,3},{9,0},{2,5},{3,6},{10,7},{11,4},{4,9},{5,10},{12... | collective-permute-start | bytes 98312 | tf_op jit(solution)/shard_map/ppermute | solution.py:379
  128.6 13.5 %collective-permute-start.22 = (f32[2,32,128]{2,1,0:T(8,128)S(1)}, f32[2,32,128]{2,1,0:T(8,128)S(1)}, u32[]{:S(2)}, u32[]{:S(2)}) collective-permute-start(f32[2,32,128]{2,1,0:T(8,128)S(1)} %get-tuple-element.62), channel_id=1, source_target_pairs={{0,2},{1,3},{8,0},{9,1},{2,6},{3,7},{10,4},{11,5},{4,10},{5,11},{1... | collective-permute-start | bytes 98312 | tf_op jit(solution)/shard_map/ppermute | solution.py:379
  137.7 4.8 %collective-permute-start.23 = (f32[2,32,128]{2,1,0:T(8,128)S(1)}, f32[2,32,128]{2,1,0:T(8,128)S(1)}, u32[]{:S(2)}, u32[]{:S(2)}) collective-permute-start(f32[2,32,128]{2,1,0:T(8,128)S(1)} %get-tuple-element.61), channel_id=1, source_target_pairs={{0,3},{1,0},{8,1},{9,2},{2,7},{3,4},{10,5},{11,6},{4,11},{5,8},{12... | collective-permute-start | bytes 98312 | tf_op jit(solution)/shard_map/ppermute | solution.py:379
  138.9 9.2 %collective-permute-start.16 = (bf16[4,128,256]{2,1,0:T(8,128)(2,1)S(1)}, bf16[4,128,256]{2,1,0:T(8,128)(2,1)S(1)}, u32[]{:S(2)}, u32[]{:S(2)}) collective-permute-start(bf16[4,128,256]{2,1,0:T(8,128)(2,1)S(1)} %slice_bitcast_fusion), channel_id=1, source_target_pairs={{0,8},{8,0},{1,9},{9,1},{2,10},{10,2},{3,11},{11,3},{4,12},{12,4},... | collective-permute-start | bytes 786440 | tf_op jit(solution)/shard_map/ppermute | solution.py:320
  148.2 6.0 %collective-permute-start.17 = (bf16[2,128,256]{2,1,0:T(8,128)(2,1)S(1)}, bf16[2,128,256]{2,1,0:T(8,128)(2,1)S(1)}, u32[]{:S(2)}, u32[]{:S(2)}) collective-permute-start(bf16[2,128,256]{2,1,0:T(8,128)(2,1)S(1)} %get-tuple-element.58), channel_id=1, source_target_pairs={{0,6},{2,0},{4,2},{6,4},{1,7},{3,1},{5,3},{7,5},{8,14},{10,8},{12,... | collective-permute-start | bytes 393224 | tf_op jit(solution)/shard_map/ppermute | solution.py:316
  149.2 5.3 %collective-permute-start.18 = (bf16[2,128,256]{2,1,0:T(8,128)(2,1)S(1)}, bf16[2,128,256]{2,1,0:T(8,128)(2,1)S(1)}, u32[]{:S(2)}, u32[]{:S(2)}) collective-permute-start(bf16[2,128,256]{2,1,0:T(8,128)(2,1)S(1)} %get-tuple-element.59), channel_id=1, source_target_pairs={{0,4},{2,6},{4,0},{6,2},{1,5},{3,7},{5,1},{7,3},{8,12},{10,14},{12... | collective-permute-start | bytes 393224 | tf_op jit(solution)/shard_map/ppermute | solution.py:316
  151.3 7.0 %collective-permute-start.19 = (bf16[2,128,256]{2,1,0:T(8,128)(2,1)S(1)}, bf16[2,128,256]{2,1,0:T(8,128)(2,1)S(1)}, u32[]{:S(2)}, u32[]{:S(2)}) collective-permute-start(bf16[2,128,256]{2,1,0:T(8,128)(2,1)S(1)} %get-tuple-element.56), channel_id=1, source_target_pairs={{0,2},{2,4},{4,6},{6,0},{1,3},{3,5},{5,7},{7,1},{8,10},{10,12},{12... | collective-permute-start | bytes 393224 | tf_op jit(solution)/shard_map/ppermute | solution.py:316
  154.2 4.1 %copy-start.5 = (s32[5]{0:T(128)S(1)}, s32[5]{0:T(128)}, u32[]{:S(2)}) copy-start(s32[5]{0:T(128)} %copy-done.4) | copy-start | bytes 64
